TPU v7x, 256 devices: a whole 4x4x8 slice. The times are simulated.
256 devices in a mesh: gx: 8 (over z), gy: 32 (over x, y, core).
Axes of the slice: x: 4, y: 4, z: 8, core: 2. Of those that a mesh axis runs over, the one named last changes fastest.
Arguments:
- charge: float32 [1024, 1024, 128], P('gx', 'gy'), may hold values from -6.1 to 6.1
- level_taps: float32 [4, 9], replicated, may hold values from 0.03 to 0.3, as said below
Outputs:
- potential: float32 [1024, 1024, 128], P('gx', 'gy')
Inputs may be any that keep to these rules, and one draw needn't show every extreme that they name: Each row is symmetric: level_taps[l, k] = level_taps[l, 8 - k].
All inputs are finite; a program needn't handle non-finite values.
Results may differ from a plain program's by a relative error of at most 0.0001.
Values sent between devices are 32-bit elements; how exact they have to be, the bound alone decides.
A program may use at most 128 MiB of HBM per device.

v0:
```python
import math

import jax
import jax.numpy as jnp
from jax import lax
from jax.sharding import PartitionSpec as P


def padded_2(array, sides, width):
    for axis, dim in sides:
        devices, length = (lax.axis_size(axis), array.shape[dim])
        up = [(i, (i + 1) % devices) for i in range(devices - 1)]
        down = [(j, i) for i, j in up]
        last = lax.slice_in_dim(array, length - width, length, axis=dim)
        initial = lax.slice_in_dim(array, 0, width, axis=dim)
        before = lax.ppermute(last, axis, up)
        after = lax.ppermute(initial, axis, down)
        array = jnp.concatenate([before, array, after], axis=dim)
    return array


def passed_along(value, axis, steps):
    count = lax.axis_size(axis)
    initial, last = (max(0, -steps), min(count, count - steps))
    return lax.ppermute(value, axis, [(source, source + steps) for source in range(initial, last)])


def tap_sum(values, weights, length, dimension):
    summed = weights[0] * lax.slice_in_dim(values, 0, length, axis=dimension)
    for offset in range(1, weights.shape[0]):
        summed = summed + weights[offset] * lax.slice_in_dim(
            values, offset, offset + length, axis=dimension
        )
    return summed


def convolve(bordered, weights, cells_x, cells_y):
    margin = (weights.shape[0] - 1) // 2
    along_x = tap_sum(bordered, weights, cells_x, 0)
    along_y = tap_sum(along_x, weights, cells_y, 1)
    cells_z = along_y.shape[2]
    deeper = jnp.pad(along_y, ((0, 0), (0, 0), (margin, margin)))
    return tap_sum(deeper, weights, cells_z, 2)


def restrict_axis(values, anchor, length, dimension):
    low_cells = lax.slice_in_dim(
        values, anchor - 1, anchor - 1 + 2 * length, stride=2, axis=dimension
    )
    middle = lax.slice_in_dim(values, anchor, anchor + 2 * length, stride=2, axis=dimension)
    high_cells = lax.slice_in_dim(values, anchor + 1, anchor + 2 * length, stride=2, axis=dimension)
    return 0.25 * low_cells + 0.5 * middle + 0.25 * high_cells


def restrict_block(bordered, cells_x, cells_y):
    margin = (bordered.shape[0] - cells_x) // 2
    coarse_x = restrict_axis(bordered, margin, cells_x // 2, 0)
    coarse_y = restrict_axis(coarse_x, margin, cells_y // 2, 1)
    deeper = jnp.pad(coarse_y, ((0, 0), (0, 0), (1, 0)))
    return restrict_axis(deeper, 1, coarse_y.shape[2] // 2, 2)


def alternate(even_cells, odd_cells, dimension):
    stacked = jnp.stack([even_cells, odd_cells], axis=dimension + 1)
    target = list(even_cells.shape)
    target[dimension] = 2 * target[dimension]
    return stacked.reshape(target)


def prolong_axis(values, length, dimension):
    low_cells = lax.slice_in_dim(values, 0, length, axis=dimension)
    high_cells = lax.slice_in_dim(values, 1, length + 1, axis=dimension)
    return alternate(low_cells, 0.5 * (low_cells + high_cells), dimension)


def prolong_block(bordered):
    cells_x = bordered.shape[0] - 1
    cells_y = bordered.shape[1] - 1
    finer_x = prolong_axis(bordered, cells_x, 0)
    finer_y = prolong_axis(finer_x, cells_y, 1)
    cells_z = finer_y.shape[2]
    deeper = jnp.pad(finer_y, ((0, 0), (0, 0), (0, 1)))
    return prolong_axis(deeper, cells_z, 2)


def gaussian_matrix(length):
    spread = max(length, 4) / 2.0
    places = jnp.arange(length, dtype=jnp.float32)
    offsets = (places[:, None] - places[None, :]) / spread
    return jnp.exp(-offsets * offsets) / (math.sqrt(math.pi) * spread)


def coarsest_field(coarse, levels):
    along_x = jnp.einsum(
        "ai,ijk->ajk", gaussian_matrix(coarse.shape[0]), coarse, precision=lax.Precision.HIGHEST
    )
    along_y = jnp.einsum(
        "bj,ajk->abk", gaussian_matrix(coarse.shape[1]), along_x, precision=lax.Precision.HIGHEST
    )
    along_z = jnp.einsum(
        "ck,abk->abc", gaussian_matrix(coarse.shape[2]), along_y, precision=lax.Precision.HIGHEST
    )
    return 2.0**levels * along_z


def extend(charges, margin):
    return padded_2(charges, (("gx", 0), ("gy", 1)), margin)


def upper_rims(current):
    rim_from_x = passed_along(current[0:1], "gx", -1)
    wider = jnp.concatenate([current, rim_from_x], 0)
    rim_from_y = passed_along(wider[:, 0:1], "gy", -1)
    return jnp.concatenate([wider, rim_from_y], 1)


def assemble(gathered, block_shape):
    cells_x, cells_y, cells_z = block_shape
    across_x = lax.axis_size("gx")
    across_y = lax.axis_size("gy")
    assembled = gathered.reshape(across_x, across_y, cells_x, cells_y, cells_z).transpose(
        0, 2, 1, 3, 4
    )
    return assembled.reshape(across_x * cells_x, across_y * cells_y, cells_z)


def local(charge, level_taps):
    levels = level_taps.shape[0]
    margin = (level_taps.shape[1] - 1) // 2
    charges = charge
    potentials = []
    for at_level in range(levels):
        cells_x, cells_y = (charges.shape[0], charges.shape[1])
        bordered = extend(charges, margin)
        potentials.append(
            2.0**at_level * convolve(bordered, level_taps[at_level], cells_x, cells_y)
        )
        charges = restrict_block(bordered, cells_x, cells_y)
    entire = assemble(
        lax.all_gather(charges[None], ("gx", "gy"), axis=0, tiled=True), charges.shape
    )
    current = coarsest_field(entire, levels)
    cells_x, cells_y, cells_z = charges.shape
    padded = jnp.pad(current, ((0, 1), (0, 1), (0, 0)))
    bordered = lax.dynamic_slice(
        padded,
        (lax.axis_index("gx") * cells_x, lax.axis_index("gy") * cells_y, 0),
        (cells_x + 1, cells_y + 1, cells_z),
    )
    for at_level in range(levels - 1, -1, -1):
        current = potentials[at_level] + prolong_block(bordered)
        if at_level > 0:
            bordered = upper_rims(current)
    return current


def solution(mesh):
    in_specs = (P("gx", "gy", None), P())
    out_specs = P("gx", "gy", None)
    return jax.shard_map(local, mesh=mesh, in_specs=in_specs, out_specs=out_specs, check_vma=False)
```

profile of v0, /device:TPU:195, one launch (start us, length us, event | category | flops | bytes accessed | tf_op | source)
XLA Modules:
  0.0 478.6 jit_solution(13744904724760783822)
XLA Ops:
  0.9 2.6 collective-permute-start
  3.5 2.6 collective-permute-start.1
  6.2 2.0 copy.84
  8.2 2.0 copy.83
  10.2 2.0 copy.85
  12.2 1.8 pad_maximum_fusion.8
  14.0 4.3 collective-permute-start.2
  18.4 1.9 collective-permute-start.3
  20.3 4.2 collective-permute-done.2
  24.5 4.4 collective-permute-done.3
  28.9 3.7 pad_maximum_fusion
  32.5 45.9 %slice.844 = f32[64,40,128]{0,2,1:T(8,128)S(1)} slice(f32[136,40,128]{0,2,1:T(8,128)} %pad_maximum_fusion), slice={[3:131:2], [0:40:1], [0:128:1]} | slice | bytes 2621440 | tf_op jit(solution)/shard_map/slice | solution.py:47
  78.4 46.3 %slice.845 = f32[64,40,128]{0,2,1:T(8,128)} slice(f32[136,40,128]{0,2,1:T(8,128)} %pad_maximum_fusion), slice={[4:132:2], [0:40:1], [0:128:1]} | slice | bytes 2621440 | tf_op jit(solution)/shard_map/slice | solution.py:50
  124.6 46.2 %slice.846 = f32[64,40,128]{0,2,1:T(8,128)} slice(f32[136,40,128]{0,2,1:T(8,128)} %pad_maximum_fusion), slice={[5:132:2], [0:40:1], [0:128:1]} | slice | bytes 2621440 | tf_op jit(solution)/shard_map/slice | solution.py:51
  170.9 3.4 multiply_add_fusion
  175.6 2.6 collective-permute-start.4
  178.2 2.6 collective-permute-start.5
  180.9 9.3 %collective-permute-done.4 = f32[4,16,64]{0,2,1:T(8,128)S(1)} collective-permute-done((f32[4,16,64]{0,2,1:T(8,128)S(1)}, f32[4,16,64]{0,2,1:T(8,128)S(1)}, u32[]{:S(2)}, u32[]{:S(2)}) %collective-permute-start.4) | collective-permute-done | bytes 16416 | tf_op jit(solution)/shard_map/ppermute | solution.py:16
  190.1 2.3 collective-permute-done.5
  192.7 3.9 collective-permute-start.6
  196.6 2.4 collective-permute-start.7
  199.0 3.9 collective-permute-done.7
  203.2 7.1 %slice.892 = f32[32,24,64]{0,2,1:T(8,128)S(1)} slice(f32[72,24,64]{0,2,1:T(8,128)S(1)} %pad_maximum_fusion.4), slice={[3:67:2], [0:24:1], [0:64:1]} | slice | bytes 393216 | tf_op jit(solution)/shard_map/slice | solution.py:47
  210.3 7.1 %slice.893 = f32[32,24,64]{0,2,1:T(8,128)S(1)} slice(f32[72,24,64]{0,2,1:T(8,128)S(1)} %pad_maximum_fusion.4), slice={[4:68:2], [0:24:1], [0:64:1]} | slice | bytes 393216 | tf_op jit(solution)/shard_map/slice | solution.py:50
  217.4 7.1 %slice.894 = f32[32,24,64]{0,2,1:T(8,128)S(1)} slice(f32[72,24,64]{0,2,1:T(8,128)S(1)} %pad_maximum_fusion.4), slice={[5:68:2], [0:24:1], [0:64:1]} | slice | bytes 393216 | tf_op jit(solution)/shard_map/slice | solution.py:51
  225.3 1.9 collective-permute-start.8
  227.2 3.4 collective-permute-start.9
  231.0 2.2 collective-permute-done.9
  233.4 3.0 collective-permute-start.10
  236.4 3.7 collective-permute-start.11
  240.1 1.9 collective-permute-done.11
  242.1 1.9 slice.940
  244.0 1.9 slice.941
  245.9 1.9 slice.942
  248.1 1.9 collective-permute-start.12
  250.0 4.3 collective-permute-start.13
  255.4 2.4 collective-permute-start.14
  257.8 5.8 %collective-permute-start.15 = (f32[24,4,16]{0,2,1:T(8,128)S(1)}, f32[24,4,16]{0,2,1:T(8,128)S(1)}, u32[]{:S(2)}, u32[]{:S(2)}) collective-permute-start(f32[24,4,16]{0,2,1:T(8,128)S(1)} %pad_maximum_fusion.25), channel_id=1, source_target_pairs={{1,0},{2,1},{3,2},{4,3},{5,4},{6,5},{7,6},{8,7},{9,8},{10,9},{11,1... | collective-permute-start | bytes 18440 | tf_op jit(solution)/shard_map/ppermute | solution.py:17
  265.6 75.8 %all-gather = f32[2048,2,8]{2,1,0:T(2,128)S(1)} all-gather(f32[8,2,8]{2,1,0:T(2,128)S(1)} %copy.86), channel_id=2, replica_groups=mesh['gx'=8,'gy'=32] {'gx','gy'}, dimensions={0}, use_global_device_ids=true | all-gather | bytes 131584 | tf_op jit(solution)/shard_map/all_gather | solution.py:140
  341.3 2.3 copy.112
  343.7 2.2 reshape.119
  348.1 5.8 %fusion.106 = f32[16,12,16]{0,2,1:T(8,128)S(1)} fusion(f32[24,12,16]{0,2,1:T(8,128)S(1)} %pad_maximum_fusion.20, f32[]{:T(128)} %bitcast.35, f32[]{:T(128)} %bitcast.34, f32[]{:T(128)} %bitcast.33, f32[]{:T(128)} %bitcast.32, f32[]{:T(128)} %bitcast.31, f32[]{:T(128)} %bitcast.30, f32[]{:T(128)} %bitcast.29, f32[]{:T(128)} %bitcast.28, f32[]{:T(128)} %bitcast.27), kind=kLoop, calls=%fused_computation.222 | loop fusion | flops 52224 | bytes 122916 | tf_op jit(solution)/shard_map/add | solution.py:31
  353.9 5.6 %fusion.145 = f32[16,4,16]{0,2,1:T(8,128)S(1)} fusion(f32[16,12,16]{0,2,1:T(8,128)S(1)} %fusion.106, f32[]{:T(128)} %bitcast.35, f32[]{:T(128)} %bitcast.34, f32[]{:T(128)} %bitcast.33, f32[]{:T(128)} %bitcast.32, f32[]{:T(128)} %bitcast.31, f32[]{:T(128)} %bitcast.30, f32[]{:T(128)} %bitcast.29, f32[]{:T(128)} %bitcast.28, f32[]{:T(128)} %bitcast.27), kind=kLoop, calls=%fused_computation.291 | loop fusion | flops 17408 | bytes 40996 | tf_op jit(solution)/shard_map/add | solution.py:31
  359.5 5.6 %fusion.134 = f32[16,4,16]{0,2,1:T(8,128)S(1)} fusion(f32[16,4,16]{0,2,1:T(8,128)S(1)} %bitcast.132, f32[16,4,16]{0,2,1:T(8,128)S(1)} %fusion.145, f32[]{:T(128)} %bitcast.35, f32[]{:T(128)} %bitcast.34, f32[]{:T(128)} %bitcast.33, f32[]{:T(128)} %bitcast.32, f32[]{:T(128)} %bitcast.31, f32[]{:T(128)} %bitcast.30, f32[]{:T(128)} %bitcast.29, f32[]{:T(128)} %bitcast.28, ...), kind=kLoop, calls=%fused_computation.278 | loop fusion | flops 19456 | bytes 12324 | tf_op jit(solution)/shard_map/add | solution.py:151
  365.1 3.7 collective-permute-start.16
  368.8 6.2 %fusion.67 = f32[32,16,32]{0,2,1:T(8,128)S(1)} fusion(f32[40,16,32]{0,2,1:T(8,128)S(1)} %pad_maximum_fusion.12, f32[]{:T(128)} %bitcast.26, f32[]{:T(128)} %bitcast.25, f32[]{:T(128)} %bitcast.24, f32[]{:T(128)} %bitcast.23, f32[]{:T(128)} %bitcast.22, f32[]{:T(128)} %bitcast.21, f32[]{:T(128)} %bitcast.20, f32[]{:T(128)} %bitcast.19, f32[]{:T(128)} %bitcast.18), kind=kLoop, calls=%fused_computation.141 | loop fusion | flops 278528 | bytes 655396 | tf_op jit(solution)/shard_map/add | solution.py:31
  375.2 2.3 collective-permute-start.17
  377.5 5.7 %fusion.98 = f32[32,8,32]{0,2,1:T(8,128)S(1)} fusion(f32[32,16,32]{0,2,1:T(8,128)S(1)} %fusion.67, f32[]{:T(128)} %bitcast.26, f32[]{:T(128)} %bitcast.25, f32[]{:T(128)} %bitcast.24, f32[]{:T(128)} %bitcast.23, f32[]{:T(128)} %bitcast.22, f32[]{:T(128)} %bitcast.21, f32[]{:T(128)} %bitcast.20, f32[]{:T(128)} %bitcast.19, f32[]{:T(128)} %bitcast.18), kind=kLoop, calls=%fused_computation.198 | loop fusion | flops 139264 | bytes 327716 | tf_op jit(solution)/shard_map/add | solution.py:31
  383.8 5.8 %fusion.90 = f32[32,8,32]{0,2,1:T(8,128)S(1)} fusion(f32[32,8,32]{0,2,1:T(8,128)S(1)} %fusion.98, f32[32,8,32]{0,1,2:T(8,128)S(1)} %bitcast.127, f32[]{:T(128)} %bitcast.26, f32[]{:T(128)} %bitcast.25, f32[]{:T(128)} %bitcast.24, f32[]{:T(128)} %bitcast.23, f32[]{:T(128)} %bitcast.22, f32[]{:T(128)} %bitcast.21, f32[]{:T(128)} %bitcast.20, f32[]{:T(128)} %bitcast.19, ...), kind=kLoop, calls=%fused_computation.189 | loop fusion | flops 155648 | bytes 98340 | tf_op jit(solution)/shard_map/add | solution.py:151
  389.6 2.8 collective-permute-start.18
  392.3 7.3 %fusion.26 = f32[64,24,64]{0,2,1:T(8,128)S(1)} fusion(f32[72,24,64]{0,2,1:T(8,128)S(1)} %pad_maximum_fusion.4, f32[]{:T(128)} %bitcast.17, f32[]{:T(128)} %bitcast.16, f32[]{:T(128)} %bitcast.15, f32[]{:T(128)} %bitcast.14, f32[]{:T(128)} %bitcast.13, f32[]{:T(128)} %bitcast.12, f32[]{:T(128)} %bitcast.11, f32[]{:T(128)} %bitcast.10, f32[]{:T(128)} %bitcast.9), kind=kLoop, calls=%fused_computation.60 | loop fusion | flops 1671168 | bytes 3932196 | tf_op jit(solution)/shard_map/add | solution.py:31
  399.7 3.9 collective-permute-start.19
  403.6 5.9 %fusion.54 = f32[64,16,64]{0,2,1:T(8,128)S(1)} fusion(f32[64,24,64]{0,2,1:T(8,128)S(1)} %fusion.26, f32[]{:T(128)} %bitcast.17, f32[]{:T(128)} %bitcast.16, f32[]{:T(128)} %bitcast.15, f32[]{:T(128)} %bitcast.14, f32[]{:T(128)} %bitcast.13, f32[]{:T(128)} %bitcast.12, f32[]{:T(128)} %bitcast.11, f32[]{:T(128)} %bitcast.10, f32[]{:T(128)} %bitcast.9), kind=kLoop, calls=%fused_computation.109 | loop fusion | flops 1114112 | bytes 2621476 | tf_op jit(solution)/shard_map/add | solution.py:31
  410.7 6.3 %fusion.46 = f32[64,16,64]{0,2,1:T(8,128)S(1)} fusion(f32[64,16,64]{0,2,1:T(8,128)S(1)} %fusion.54, f32[64,16,64]{0,1,2:T(8,128)S(1)} %bitcast.122, f32[]{:T(128)} %bitcast.17, f32[]{:T(128)} %bitcast.16, f32[]{:T(128)} %bitcast.15, f32[]{:T(128)} %bitcast.14, f32[]{:T(128)} %bitcast.13, f32[]{:T(128)} %bitcast.12, f32[]{:T(128)} %bitcast.11, f32[]{:T(128)} %bitcast.10, ...), kind=kLoop, calls=%fused_computation.100 | loop fusion | flops 1245184 | bytes 786468 | tf_op jit(solution)/shard_map/add | solution.py:151
  417.0 3.6 collective-permute-start.20
  420.6 25.6 %fusion = f32[128,40,128]{0,2,1:T(8,128)S(1)} fusion(f32[136,40,128]{0,2,1:T(8,128)} %pad_maximum_fusion, f32[]{:T(128)} %bitcast.8, f32[]{:T(128)} %bitcast.7, f32[]{:T(128)} %bitcast.6, f32[]{:T(128)} %bitcast.5, f32[]{:T(128)} %bitcast.4, f32[]{:T(128)} %bitcast.3, f32[]{:T(128)} %bitcast.2, f32[]{:T(128)} %bitcast.1, f32[]{:T(128)} %bitcast), kind=kLoop, calls=%fused_computation.2 | loop fusion | flops 11141120 | bytes 26214436 | tf_op jit(solution)/shard_map/add | solution.py:31
  446.3 2.3 collective-permute-start.21
  448.6 7.6 %fusion.8 = f32[128,32,128]{0,2,1:T(8,128)S(1)} fusion(f32[128,40,128]{0,2,1:T(8,128)S(1)} %fusion, f32[]{:T(128)} %bitcast.8, f32[]{:T(128)} %bitcast.7, f32[]{:T(128)} %bitcast.6, f32[]{:T(128)} %bitcast.5, f32[]{:T(128)} %bitcast.4, f32[]{:T(128)} %bitcast.3, f32[]{:T(128)} %bitcast.2, f32[]{:T(128)} %bitcast.1, f32[]{:T(128)} %bitcast), kind=kLoop, calls=%fused_computation.20 | loop fusion | flops 8912896 | bytes 20971556 | tf_op jit(solution)/shard_map/add | solution.py:31
  457.8 2.0 copy.105
  460.1 1.5 pad_maximum_fusion.1
  461.5 2.2 copy.106
  464.1 1.2 copy.108
  465.3 10.1 %copy_add_fusion = f32[128,32,128]{0,2,1:T(8,128)} fusion(f32[128,32,128]{0,1,2:T(8,128)S(1)} %bitcast.117, f32[128,32,128]{0,2,1:T(8,128)S(1)} %fusion.8, f32[]{:T(128)} %bitcast.8, f32[]{:T(128)} %bitcast.7, f32[]{:T(128)} %bitcast.6, f32[]{:T(128)} %bitcast.5, f32[]{:T(128)} %bitcast.4, f32[]{:T(128)} %bitcast.3, f32[]{:T(128)} %bitcast.2, f32[]{:T(128)} %bitcast.1, ...), kind=kLoop, calls=%fused_computation.38 | loop fusion | flops 9437184 | bytes 6291492 | tf_op jit(solution)/shard_map/add | solution.py:151
  475.4 3.0 copy.110
  (106 shorter events, 13.5 us)
Async XLA Ops:
  0.9 7.3 %collective-permute-start = (f32[4,32,128]{2,1,0:T(8,128)S(1)}, f32[4,32,128]{2,1,0:T(8,128)S(1)}, u32[]{:S(2)}, u32[]{:S(2)}) collective-permute-start(f32[4,32,128]{2,1,0:T(8,128)S(1)} %get-tuple-element.7), channel_id=1, source_target_pairs={{0,32},{32,64},{64,96},{96,128},{128,160},{160,192},{192,224},{1,3... | collective-permute-start | bytes 196616 | tf_op jit(solution)/shard_map/ppermute | solution.py:16
  3.5 6.7 %collective-permute-start.1 = (f32[4,32,128]{2,1,0:T(8,128)S(1)}, f32[4,32,128]{2,1,0:T(8,128)S(1)}, u32[]{:S(2)}, u32[]{:S(2)}) collective-permute-start(f32[4,32,128]{2,1,0:T(8,128)S(1)} %get-tuple-element.8), channel_id=1, source_target_pairs={{32,0},{64,32},{96,64},{128,96},{160,128},{192,160},{224,192},{33,... | collective-permute-start | bytes 196616 | tf_op jit(solution)/shard_map/ppermute | solution.py:17
  12.2 16.7 %copy-start = (f32[4,32,128]{0,2,1:T(8,128)S(1)}, f32[4,32,128]{0,2,1:T(8,128)}, u32[]{:S(2)}) copy-start(f32[4,32,128]{0,2,1:T(8,128)} %copy.83) | copy-start | bytes 196612
  12.2 16.7 %copy-start.1 = (f32[4,32,128]{0,2,1:T(8,128)S(1)}, f32[4,32,128]{0,2,1:T(8,128)}, u32[]{:S(2)}) copy-start(f32[4,32,128]{0,2,1:T(8,128)} %copy.85) | copy-start | bytes 196612
  14.0 10.4 %collective-permute-start.2 = (f32[136,4,128]{0,2,1:T(8,128)S(1)}, f32[136,4,128]{0,2,1:T(8,128)S(1)}, u32[]{:S(2)}, u32[]{:S(2)}) collective-permute-start(f32[136,4,128]{0,2,1:T(8,128)S(1)} %get-tuple-element.5), channel_id=1, source_target_pairs={{0,1},{1,2},{2,3},{3,4},{4,5},{5,6},{6,7},{7,8},{8,9},{9,10},{10,1... | collective-permute-start | bytes 835592 | tf_op jit(solution)/shard_map/ppermute | solution.py:16
  18.4 10.5 %collective-permute-start.3 = (f32[136,4,128]{0,2,1:T(8,128)S(1)}, f32[136,4,128]{0,2,1:T(8,128)S(1)}, u32[]{:S(2)}, u32[]{:S(2)}) collective-permute-start(f32[136,4,128]{0,2,1:T(8,128)S(1)} %get-tuple-element.6), channel_id=1, source_target_pairs={{1,0},{2,1},{3,2},{4,3},{5,4},{6,5},{7,6},{8,7},{9,8},{10,9},{11,1... | collective-permute-start | bytes 835592 | tf_op jit(solution)/shard_map/ppermute | solution.py:17
  175.6 14.6 %collective-permute-start.4 = (f32[4,16,64]{0,2,1:T(8,128)S(1)}, f32[4,16,64]{0,2,1:T(8,128)S(1)}, u32[]{:S(2)}, u32[]{:S(2)}) collective-permute-start(f32[4,16,64]{0,2,1:T(8,128)S(1)} %get-tuple-element.15), channel_id=1, source_target_pairs={{0,32},{32,64},{64,96},{96,128},{128,160},{160,192},{192,224},{1,3... | collective-permute-start | bytes 49160 | tf_op jit(solution)/shard_map/ppermute | solution.py:16
  178.2 14.3 %collective-permute-start.5 = (f32[4,16,64]{0,2,1:T(8,128)S(1)}, f32[4,16,64]{0,2,1:T(8,128)S(1)}, u32[]{:S(2)}, u32[]{:S(2)}) collective-permute-start(f32[4,16,64]{0,2,1:T(8,128)S(1)} %get-tuple-element.16), channel_id=1, source_target_pairs={{32,0},{64,32},{96,64},{128,96},{160,128},{192,160},{224,192},{33,... | collective-permute-start | bytes 49160 | tf_op jit(solution)/shard_map/ppermute | solution.py:17
  192.7 6.3 %collective-permute-start.6 = (f32[72,4,64]{0,2,1:T(8,128)S(1)}, f32[72,4,64]{0,2,1:T(8,128)S(1)}, u32[]{:S(2)}, u32[]{:S(2)}) collective-permute-start(f32[72,4,64]{0,2,1:T(8,128)S(1)} %get-tuple-element.9), channel_id=1, source_target_pairs={{0,1},{1,2},{2,3},{3,4},{4,5},{5,6},{6,7},{7,8},{8,9},{9,10},{10,1... | collective-permute-start | bytes 221192 | tf_op jit(solution)/shard_map/ppermute | solution.py:16
  196.6 6.3 %collective-permute-start.7 = (f32[72,4,64]{0,2,1:T(8,128)S(1)}, f32[72,4,64]{0,2,1:T(8,128)S(1)}, u32[]{:S(2)}, u32[]{:S(2)}) collective-permute-start(f32[72,4,64]{0,2,1:T(8,128)S(1)} %get-tuple-element.10), channel_id=1, source_target_pairs={{1,0},{2,1},{3,2},{4,3},{5,4},{6,5},{7,6},{8,7},{9,8},{10,9},{11,1... | collective-permute-start | bytes 221192 | tf_op jit(solution)/shard_map/ppermute | solution.py:17
  225.3 5.7 %collective-permute-start.8 = (f32[4,8,32]{0,2,1:T(8,128)S(1)}, f32[4,8,32]{0,2,1:T(8,128)S(1)}, u32[]{:S(2)}, u32[]{:S(2)}) collective-permute-start(f32[4,8,32]{0,2,1:T(8,128)S(1)} %get-tuple-element.25), channel_id=1, source_target_pairs={{0,32},{32,64},{64,96},{96,128},{128,160},{160,192},{192,224},{1,3... | collective-permute-start | bytes 12296 | tf_op jit(solution)/shard_map/ppermute | solution.py:16
  227.2 6.0 %collective-permute-start.9 = (f32[4,8,32]{0,2,1:T(8,128)S(1)}, f32[4,8,32]{0,2,1:T(8,128)S(1)}, u32[]{:S(2)}, u32[]{:S(2)}) collective-permute-start(f32[4,8,32]{0,2,1:T(8,128)S(1)} %get-tuple-element.26), channel_id=1, source_target_pairs={{32,0},{64,32},{96,64},{128,96},{160,128},{192,160},{224,192},{33,... | collective-permute-start | bytes 12296 | tf_op jit(solution)/shard_map/ppermute | solution.py:17
  233.4 6.7 %collective-permute-start.10 = (f32[40,4,32]{0,2,1:T(8,128)S(1)}, f32[40,4,32]{0,2,1:T(8,128)S(1)}, u32[]{:S(2)}, u32[]{:S(2)}) collective-permute-start(f32[40,4,32]{0,2,1:T(8,128)S(1)} %get-tuple-element.23), channel_id=1, source_target_pairs={{0,1},{1,2},{2,3},{3,4},{4,5},{5,6},{6,7},{7,8},{8,9},{9,10},{10,1... | collective-permute-start | bytes 61448 | tf_op jit(solution)/shard_map/ppermute | solution.py:16
  236.4 17.9 %copy-start.2 = (f32[4,9]{1,0:T(4,128)S(1)}, f32[4,9]{1,0:T(4,128)}, u32[]{:S(2)}) copy-start(f32[4,9]{1,0:T(4,128)} %param.3) | copy-start | bytes 436
  236.4 5.6 %collective-permute-start.11 = (f32[40,4,32]{0,2,1:T(8,128)S(1)}, f32[40,4,32]{0,2,1:T(8,128)S(1)}, u32[]{:S(2)}, u32[]{:S(2)}) collective-permute-start(f32[40,4,32]{0,2,1:T(8,128)S(1)} %get-tuple-element.24), channel_id=1, source_target_pairs={{1,0},{2,1},{3,2},{4,3},{5,4},{6,5},{7,6},{8,7},{9,8},{10,9},{11,1... | collective-permute-start | bytes 61448 | tf_op jit(solution)/shard_map/ppermute | solution.py:17
  248.1 6.9 %collective-permute-start.12 = (f32[4,4,16]{0,2,1:T(8,128)S(1)}, f32[4,4,16]{0,2,1:T(8,128)S(1)}, u32[]{:S(2)}, u32[]{:S(2)}) collective-permute-start(f32[4,4,16]{0,2,1:T(8,128)S(1)} %get-tuple-element.31), channel_id=1, source_target_pairs={{0,32},{32,64},{64,96},{96,128},{128,160},{160,192},{192,224},{1,3... | collective-permute-start | bytes 3080 | tf_op jit(solution)/shard_map/ppermute | solution.py:16
  250.0 5.3 %collective-permute-start.13 = (f32[4,4,16]{0,2,1:T(8,128)S(1)}, f32[4,4,16]{0,2,1:T(8,128)S(1)}, u32[]{:S(2)}, u32[]{:S(2)}) collective-permute-start(f32[4,4,16]{0,2,1:T(8,128)S(1)} %get-tuple-element.32), channel_id=1, source_target_pairs={{32,0},{64,32},{96,64},{128,96},{160,128},{192,160},{224,192},{33,... | collective-permute-start | bytes 3080 | tf_op jit(solution)/shard_map/ppermute | solution.py:17
  255.4 8.9 %collective-permute-start.14 = (f32[24,4,16]{0,2,1:T(8,128)S(1)}, f32[24,4,16]{0,2,1:T(8,128)S(1)}, u32[]{:S(2)}, u32[]{:S(2)}) collective-permute-start(f32[24,4,16]{0,2,1:T(8,128)S(1)} %pad_maximum_fusion.25), channel_id=1, source_target_pairs={{0,1},{1,2},{2,3},{3,4},{4,5},{5,6},{6,7},{7,8},{8,9},{9,10},{10,1... | collective-permute-start | bytes 18440 | tf_op jit(solution)/shard_map/ppermute | solution.py:16
  257.8 6.6 %collective-permute-start.15 = (f32[24,4,16]{0,2,1:T(8,128)S(1)}, f32[24,4,16]{0,2,1:T(8,128)S(1)}, u32[]{:S(2)}, u32[]{:S(2)}) collective-permute-start(f32[24,4,16]{0,2,1:T(8,128)S(1)} %pad_maximum_fusion.25), channel_id=1, source_target_pairs={{1,0},{2,1},{3,2},{4,3},{5,4},{6,5},{7,6},{8,7},{9,8},{10,9},{11,1... | collective-permute-start | bytes 18440 | tf_op jit(solution)/shard_map/ppermute | solution.py:17
  365.1 10.0 %collective-permute-start.16 = (f32[1,4,16]{0,2,1:T(8,128)S(1)}, f32[1,4,16]{0,2,1:T(8,128)S(1)}, u32[]{:S(2)}, u32[]{:S(2)}) collective-permute-start(f32[1,4,16]{0,2,1:T(8,128)S(1)} %bitcast.128), channel_id=1, source_target_pairs={{32,0},{64,32},{96,64},{128,96},{160,128},{192,160},{224,192},{33,... | collective-permute-start | bytes 776 | tf_op jit(solution)/shard_map/ppermute | solution.py:25
  375.2 8.1 %collective-permute-start.17 = (f32[17,1,16]{0,2,1:T(8,128)S(1)}, f32[17,1,16]{0,2,1:T(8,128)S(1)}, u32[]{:S(2)}, u32[]{:S(2)}) collective-permute-start(f32[17,1,16]{0,2,1:T(8,128)S(1)} %pad_maximum_fusion.29), channel_id=1, source_target_pairs={{1,0},{2,1},{3,2},{4,3},{5,4},{6,5},{7,6},{8,7},{9,8},{10,9},{11,1... | collective-permute-start | bytes 3272 | tf_op jit(solution)/shard_map/ppermute | solution.py:25
  389.6 10.1 %collective-permute-start.18 = (f32[1,8,32]{0,2,1:T(8,128)S(1)}, f32[1,8,32]{0,2,1:T(8,128)S(1)}, u32[]{:S(2)}, u32[]{:S(2)}) collective-permute-start(f32[1,8,32]{0,2,1:T(8,128)S(1)} %bitcast.123), channel_id=1, source_target_pairs={{32,0},{64,32},{96,64},{128,96},{160,128},{192,160},{224,192},{33,... | collective-permute-start | bytes 3080 | tf_op jit(solution)/shard_map/ppermute | solution.py:25
  399.7 9.8 %collective-permute-start.19 = (f32[33,1,32]{0,2,1:T(8,128)S(1)}, f32[33,1,32]{0,2,1:T(8,128)S(1)}, u32[]{:S(2)}, u32[]{:S(2)}) collective-permute-start(f32[33,1,32]{0,2,1:T(8,128)S(1)} %pad_maximum_fusion.28), channel_id=1, source_target_pairs={{1,0},{2,1},{3,2},{4,3},{5,4},{6,5},{7,6},{8,7},{9,8},{10,9},{11,1... | collective-permute-start | bytes 12680 | tf_op jit(solution)/shard_map/ppermute | solution.py:25
  417.0 29.2 %collective-permute-start.20 = (f32[1,16,64]{0,2,1:T(8,128)S(1)}, f32[1,16,64]{0,2,1:T(8,128)S(1)}, u32[]{:S(2)}, u32[]{:S(2)}) collective-permute-start(f32[1,16,64]{0,2,1:T(8,128)S(1)} %bitcast.118), channel_id=1, source_target_pairs={{32,0},{64,32},{96,64},{128,96},{160,128},{192,160},{224,192},{33,... | collective-permute-start | bytes 12296 | tf_op jit(solution)/shard_map/ppermute | solution.py:25
  446.3 10.0 %collective-permute-start.21 = (f32[65,1,64]{0,2,1:T(8,128)S(1)}, f32[65,1,64]{0,2,1:T(8,128)S(1)}, u32[]{:S(2)}, u32[]{:S(2)}) collective-permute-start(f32[65,1,64]{0,2,1:T(8,128)S(1)} %pad_maximum_fusion.24), channel_id=1, source_target_pairs={{1,0},{2,1},{3,2},{4,3},{5,4},{6,5},{7,6},{8,7},{9,8},{10,9},{11,1... | collective-permute-start | bytes 49928 | tf_op jit(solution)/shard_map/ppermute | solution.py:25
where the time goes:
time: 488 us; the launch traced here: 479 us
  local copies, waits for them, and re-layouts  190 us (39%)
  other arithmetic  113 us (23%)
  blocking collectives  75.8 us (16%)
  starting transfers between devices  68.1 us (14%)
  waiting for transfers between devices  29 us (6%)
    all_gather x1, blocking collectives, local(): lax.all_gather(charges[None], ('gx', 'gy'), axis=0, tiled=True)  75.8 us
    add x8, other arithmetic, tap_sum(): summed + weights[offset] * lax.slice_in_dim(values, offset, offset + leng...  69.7 us
    slice x8, local copies, waits for them, and re-layouts, restrict_axis(): lax.slice_in_dim(values, anchor, anchor + 2 * length, stride=2, axis=dime...  55.9 us
    slice x8, local copies, waits for them, and re-layouts, restrict_axis(): lax.slice_in_dim(values, anchor + 1, anchor + 2 * length, stride=2, axis=...  55.9 us
    slice x8, local copies, waits for them, and re-layouts, restrict_axis(): lax.slice_in_dim(values, anchor - 1, anchor - 1 + 2 * length, stride=2, a...  55.5 us
    add x4, other arithmetic, local(): current = potentials[at_level] + prolong_block(bordered)  27.8 us
    ppermute x8, starting transfers between devices, padded_2(): after = lax.ppermute(initial, axis, down)  26.7 us
    ppermute x8, starting transfers between devices, padded_2(): before = lax.ppermute(last, axis, up)  22.7 us
  transfers between devices with their start and end apart: 22, of which 10 were waited for; matrix products, arithmetic and copies ran while one was open for 13% of the time, Pallas kernels for 0%

commit v1 on v0

v1 whole, which is shorter than its diff:
```python
import functools
import math

import jax
import jax.numpy as jnp
from jax import lax
from jax.experimental import pallas as pl
from jax.experimental.pallas import tpu as pltpu
from jax.sharding import PartitionSpec as P

F32 = jnp.float32
BF16 = jnp.bfloat16
HIGHEST = lax.Precision.HIGHEST
MESH = pl.DeviceIdType.MESH

CX, CY, CZ = 128, 32, 128
REACH = 4
LANES = {1: (0, 64), 2: (64, 32), 3: (96, 16), 4: (112, 8)}
NXL = {1: 64, 2: 32, 3: 16, 4: 8}
NYL = {1: 16, 2: 8, 3: 4, 4: 2}
ROWS = {1: 24, 2: 16, 3: 8, 4: 8}


def iota(shape, dim):
    return lax.broadcasted_iota(jnp.int32, shape, dim)


def gauss(distance, length):
    spread = max(length, 4) / 2.0
    scaled = distance.astype(F32) / spread
    return jnp.exp(-scaled * scaled) / (math.sqrt(math.pi) * spread)


def split(value):
    high = value.astype(BF16)
    return high, (value - high.astype(F32)).astype(BF16)


def stacked(matrix):
    high, low = split(matrix)
    return jnp.concatenate([high, high, low], axis=0)


def product(value, weights):
    high, low = split(value)
    both = jnp.concatenate([high, low, high], axis=1)
    return jnp.dot(both, weights, preferred_element_type=F32)


def toeplitz(taps, level, shape, offset):
    matrix = jnp.zeros(shape, F32)
    for k in range(2 * REACH + 1):
        matrix = jnp.where(offset == k - REACH, taps[level, k], matrix)
    return matrix


def coarse_z(taps):
    a, c = iota((CZ, CZ), 0), iota((CZ, CZ), 1)
    down = jnp.zeros((CZ, CZ), F32)
    mix = jnp.zeros((CZ, CZ), F32)
    for level, (first, cells) in LANES.items():
        step = 2**level
        here = (c >= first) & (c < first + cells)
        weight = jnp.maximum(0, step - jnp.abs(a - step * (c - first)))
        down = jnp.where(here, weight.astype(F32) * 2.0 ** (-5 * level), down)
        inside = here & (a >= first) & (a < first + cells)
        if level < 4:
            block = toeplitz(taps, level, (CZ, CZ), a - c)
        else:
            block = gauss(a - c, cells)
        mix = jnp.where(inside, block, mix)
    return jnp.dot(down, mix, precision=HIGHEST, preferred_element_type=F32)


def prolong_z():
    r, a = iota((CZ, CZ), 0), iota((CZ, CZ), 1)
    up = jnp.zeros((CZ, CZ), F32)
    for level, (first, cells) in LANES.items():
        step = 2**level
        here = (r >= first) & (r < first + cells)
        weight = jnp.maximum(0, step - jnp.abs(a - step * (r - first)))
        up = jnp.where(here, weight.astype(F32) * 2.0**-level, up)
    return up.astype(BF16)


def weighted(pieces, weights):
    total = weights[REACH] * pieces[REACH]
    for k in range(REACH):
        total = total + weights[k] * (pieces[k] + pieces[2 * REACH - k])
    return total


def kernel(
    across_x, across_y, taps, q, out,
    E, C, T1, T2, T3, T4, A1, A2, A3, A4, B1, B2, B3, U1, U2, U3, E4, G3, G2, G1, G0,
    XS, XR, YS, YR, GA, GB, WZ, W0, PZ, E1Z,
    in_sem, y0_send, y0_recv, x0_send, x0_recv, cx_send, cx_recv, cy_send, cy_recv,
    c2_send, c2_recv, ga_send, ga_recv, gb_send, gb_recv,
):
    me_x, me_y = lax.axis_index("gx"), lax.axis_index("gy")
    first_x, last_x = me_x == 0, me_x == across_x - 1
    first_y, last_y = me_y == 0, me_y == across_y - 1
    A, B, U, T = {1: A1, 2: A2, 3: A3}, {1: B1, 2: B2, 3: B3}, {1: U1, 2: U2, 3: U3}, {2: T2, 3: T3, 4: T4}

    barrier = pltpu.get_barrier_semaphore()

    def greet_y(step, carry):
        pl.semaphore_signal(barrier, inc=1, device_id={"gy": lax.rem(me_y + step, across_y)}, device_id_type=MESH)
        return carry

    def greet_x(step, carry):
        pl.semaphore_signal(barrier, inc=1, device_id={"gx": lax.rem(me_x + step, across_x)}, device_id_type=MESH)
        return carry

    lax.fori_loop(1, across_y, greet_y, 0)
    lax.fori_loop(1, across_x, greet_x, 0)

    parts = 4
    depth = CX // parts
    loads = [
        pltpu.make_async_copy(
            q.at[pl.ds(i * depth, depth)], E.at[pl.ds(i * depth, depth), pl.ds(8, CY)], in_sem.at[i]
        )
        for i in range(parts)
    ]
    for load in loads:
        load.start()

    WZ[...] = stacked(coarse_z(taps))
    W0[...] = stacked(toeplitz(taps, 0, (CZ, CZ), iota((CZ, CZ), 0) - iota((CZ, CZ), 1)))
    rise = prolong_z()
    PZ[...] = jnp.concatenate([rise, rise], axis=0)

    def blank(ref, count, *spans):
        def body(i, carry):
            for start, size in spans:
                ref[i, pl.ds(start, size), :] = jnp.zeros((size, CZ), F32)
            return carry
        lax.fori_loop(0, count, body, 0)

    blank(T1, 65, (0, 8), (40, 16))
    blank(T2, 33, (0, 8), (32, 8))
    blank(T3, 17, (0, 8))
    blank(T4, 9, (0, 8), (16, 8))
    for level in (1, 2, 3):
        blank(B[level], NXL[level] + 1, (0, 8), *(((16, 8),) if level == 3 else ()))
        rows = ROWS[level]
        A[level][0:4] = jnp.zeros((4, rows, CZ), F32)
        A[level][NXL[level] + 5 : NXL[level] + 9] = jnp.zeros((4, rows, CZ), F32)

    @pl.when(first_y)
    def _():
        E[:, 4:8, :] = jnp.zeros((CX, 4, CZ), F32)
        YR[0, :, 0:5, :] = jnp.zeros((65, 5, CZ), F32)

    @pl.when(last_y)
    def _():
        E[:, 40:44, :] = jnp.zeros((CX, 4, CZ), F32)
        YR[1, :, 0:5, :] = jnp.zeros((65, 5, CZ), F32)

    @pl.when(me_y < 2)
    def _():
        YR[0, 0:17, 5:6, :] = jnp.zeros((17, 1, CZ), F32)

    @pl.when(me_y >= across_y - 2)
    def _():
        YR[1, 0:17, 5:6, :] = jnp.zeros((17, 1, CZ), F32)

    @pl.when(first_x)
    def _():
        C[0:4] = jnp.zeros((4, CY, CZ), F32)
        XR[0] = jnp.zeros((5, 24, CZ), F32)

    @pl.when(last_x)
    def _():
        C[CX + 4 : CX + 8] = jnp.zeros((4, CY, CZ), F32)
        XR[1] = jnp.zeros((5, 24, CZ), F32)

    pl.semaphore_wait(barrier, across_x + across_y - 2)

    def remote(src, dst, send, recv, **target):
        return pltpu.make_async_remote_copy(
            src_ref=src, dst_ref=dst, send_sem=send, recv_sem=recv, device_id=target, device_id_type=MESH
        )

    above_y, below_y = lax.rem(me_y + 1, across_y), lax.rem(me_y + across_y - 1, across_y)
    above_x, below_x = lax.rem(me_x + 1, across_x), lax.rem(me_x + across_x - 1, across_x)

    y0_up = remote(q.at[:, pl.ds(CY - 4, 4)], E.at[:, pl.ds(4, 4)], y0_send.at[0], y0_recv.at[0], gy=above_y)
    y0_down = remote(q.at[:, pl.ds(0, 4)], E.at[:, pl.ds(40, 4)], y0_send.at[1], y0_recv.at[1], gy=below_y)
    pl.when(jnp.logical_not(last_y))(y0_up.start)
    pl.when(jnp.logical_not(first_y))(y0_down.start)

    for load in loads:
        load.wait()

    T1[0, 8:40, :] = 2.0 * E[0, 8:40, :] + E[1, 8:40, :]
    T1[64, 8:40, :] = E[CX - 1, 8:40, :]

    def down_x(i, carry):
        T1[i, 8:40, :] = E[2 * i - 1, 8:40, :] + 2.0 * E[2 * i, 8:40, :] + E[2 * i + 1, 8:40, :]
        return carry

    lax.fori_loop(1, 64, down_x, 0, unroll=3)

    def down_yz(i, carry):
        at = pl.ds(i * 5, 5)
        value = (
            T1[at, pl.ds(7, 24, stride=2), :]
            + 2.0 * T1[at, pl.ds(8, 24, stride=2), :]
            + T1[at, pl.ds(9, 24, stride=2), :]
        )
        A1[pl.ds(4 + i * 5, 5)] = product(value.reshape(5 * 24, CZ), WZ[...]).reshape(5, 24, CZ)
        return carry

    lax.fori_loop(0, 13, down_yz, 0)

    for level in (2, 3, 4):
        finer, mid = A[level - 1], T[level]
        coarser, shift = (A[level], 4) if level < 4 else (A4, 0)
        inner, rows = ROWS[level - 1], ROWS[level]

        def down(i, carry, finer=finer, mid=mid, coarser=coarser, shift=shift, inner=inner, rows=rows):
            mid[i, pl.ds(8, inner), :] = finer[2 * i + 3] + 2.0 * finer[2 * i + 4] + finer[2 * i + 5]
            coarser[i + shift] = (
                mid[i, pl.ds(7, rows, stride=2), :]
                + 2.0 * mid[i, pl.ds(8, rows, stride=2), :]
                + mid[i, pl.ds(9, rows, stride=2), :]
            )
            return carry

        lax.fori_loop(0, NXL[level] + 1, down, 0)

    lane8 = iota((8, CZ), 1)
    message = jnp.zeros((8, CZ), F32)
    for x in range(9):
        value = jnp.where((lane8 >= 112) & (lane8 < 120), A4[x], 0.0)
        message = message + pltpu.roll(value, (8 * x - 112) % CZ, 1)
    GA[me_y] = message

    def send_a(step, carry):
        remote(GA.at[me_y], GA.at[me_y], ga_send, ga_recv, gy=lax.rem(me_y + step, across_y)).start()
        return carry

    lax.fori_loop(1, across_y, send_a, 0)

    @pl.when(last_x)
    def _():
        for level in (1, 2, 3):
            A[level][NXL[level] + 4] = jnp.zeros((ROWS[level], CZ), F32)

    for way in (0, 1):
        for i in range(5):
            at = {level: (NXL[level] if way == 0 else 4) + i for level in (1, 2, 3)}
            wide = A1[at[1]]
            lane = iota((24, CZ), 1)
            XS[way, i] = jnp.where(lane < 64, wide, 0.0)
            lane = iota((16, CZ), 1)
            XS[way, i, 0:16, :] = jnp.where(lane >= 64, A2[at[2]], XS[way, i, 0:16, :])
            lane = iota((8, CZ), 1)
            XS[way, i, 0:8, :] = jnp.where(lane >= 96, A3[at[3]], XS[way, i, 0:8, :])
    cx_up = remote(XS.at[0], XR.at[0], cx_send.at[0], cx_recv.at[0], gx=above_x)
    cx_down = remote(XS.at[1], XR.at[1], cx_send.at[1], cx_recv.at[1], gx=below_x)
    pl.when(jnp.logical_not(last_x))(cx_up.start)
    pl.when(jnp.logical_not(first_x))(cx_down.start)

    w0 = [taps[0, k] for k in range(2 * REACH + 1)]

    def mid_y(i, carry):
        C[4 + i, 8:24, :] = weighted([E[i, 12 + k : 28 + k, :] for k in range(9)], w0)
        return carry

    lax.fori_loop(0, CX, mid_y, 0, unroll=2)

    pl.when(jnp.logical_not(first_x))(cx_up.wait_recv)
    pl.when(jnp.logical_not(last_x))(cx_down.wait_recv)
    for level in (1, 2, 3):
        array, rows, n = A[level], ROWS[level], NXL[level]
        array[0:4] = XR[0, 0:4, 0:rows, :]
        array[4] = array[4] + XR[0, 4, 0:rows, :]
        array[n + 4] = array[n + 4] + XR[1, 0, 0:rows, :]
        array[n + 5 : n + 9] = XR[1, 1:5, 0:rows, :]
        wl = [taps[level, k] for k in range(2 * REACH + 1)]

        def along_x(i, carry, array=array, target=B[level], rows=rows, wl=wl):
            target[i, pl.ds(8, rows), :] = weighted([array[i + k] for k in range(9)], wl)
            return carry

        lax.fori_loop(0, n + 1, along_x, 0)

        @pl.when(last_x)
        def _(target=B[level], rows=rows, n=n):
            target[n, pl.ds(8, rows), :] = jnp.zeros((rows, CZ), F32)

        @pl.when(last_y)
        def _(target=B[level], level=level, n=n):
            target[:, pl.ds(8 + NYL[level], 1), :] = jnp.zeros((n + 1, 1, CZ), F32)

    def pack(x, levels):
        for way in (0, 1):
            lane = iota((8, CZ), 1)
            value = None
            for level in levels:
                start = 8 + (NYL[level] - 4 if way == 0 else 0)
                piece = B[level][x, pl.ds(start, 8), :]
                value = piece if value is None else jnp.where(lane >= LANES[level][0], piece, value)
            YS[way, x] = value

    lax.fori_loop(0, 17, lambda x, c: (pack(x, (1, 2, 3)), c)[1], 0)
    lax.fori_loop(17, 33, lambda x, c: (pack(x, (1, 2)), c)[1], 0)
    lax.fori_loop(33, 65, lambda x, c: (pack(x, (1,)), c)[1], 0)
    rows5 = pl.ds(0, 5)
    cy_up = remote(YS.at[0, :, rows5], YR.at[0, :, rows5], cy_send.at[0], cy_recv.at[0], gy=above_y)
    cy_down = remote(YS.at[1, :, rows5], YR.at[1, :, rows5], cy_send.at[1], cy_recv.at[1], gy=below_y)
    pl.when(jnp.logical_not(last_y))(cy_up.start)
    pl.when(jnp.logical_not(first_y))(cy_down.start)
    near, far = pl.ds(0, 17), pl.ds(5, 1)
    c2_up = remote(
        YS.at[0, near, pl.ds(4, 1)], YR.at[0, near, far], c2_send.at[0], c2_recv.at[0],
        gy=lax.rem(me_y + 2, across_y),
    )
    c2_down = remote(
        YS.at[1, near, pl.ds(0, 1)], YR.at[1, near, far], c2_send.at[1], c2_recv.at[1],
        gy=lax.rem(me_y + across_y - 2, across_y),
    )
    pl.when(me_y < across_y - 2)(c2_up.start)
    pl.when(me_y >= 2)(c2_down.start)

    others = pl.ds(0, across_y - 1)
    pltpu.make_async_copy(GA.at[others], GA.at[others], ga_recv).wait()
    row, col = iota((8, 8 * across_y), 0), iota((8, 8 * across_y), 1)
    spot, place = 2 * me_y + row, 2 * (col // 8) + col % 8
    valid = (row < 3) & (spot < 2 * across_y) & (col % 8 < 3) & (place < 2 * across_y)
    along = jnp.where(valid, gauss(spot - place, 2 * across_y), 0.0)
    value = jnp.dot(along, GA[...].reshape(8 * across_y, CZ), precision=HIGHEST, preferred_element_type=F32)
    lane16, row16 = iota((16, CZ), 1), iota((16, CZ), 0)
    keep = (lane16 // 8 == row16) & (row16 < 9)
    spread = jnp.concatenate(
        [jnp.where(keep, jnp.broadcast_to(value[y : y + 1], (16, CZ)), 0.0) for y in range(3)], axis=1
    )
    r, c = iota((3 * CZ, CZ), 0), iota((3 * CZ, CZ), 1)
    pick = (c == 8 * (r // CZ) + r % 8).astype(F32)
    GB[me_x] = jnp.dot(spread, pick, precision=HIGHEST, preferred_element_type=F32)

    def send_b(step, carry):
        remote(GB.at[me_x], GB.at[me_x], gb_send, gb_recv, gx=lax.rem(me_x + step, across_x)).start()
        return carry

    lax.fori_loop(1, across_x, send_b, 0)

    pl.when(jnp.logical_not(first_y))(y0_up.wait_recv)
    pl.when(jnp.logical_not(last_y))(y0_down.wait_recv)

    def outer_y(i, carry):
        C[4 + i, 0:8, :] = weighted([E[i, 4 + k : 12 + k, :] for k in range(9)], w0)
        C[4 + i, 24:32, :] = weighted([E[i, 28 + k : 36 + k, :] for k in range(9)], w0)
        return carry

    lax.fori_loop(0, 4, outer_y, 0)
    lax.fori_loop(CX - 4, CX, outer_y, 0)
    x0_up = remote(C.at[pl.ds(CX, 4)], C.at[pl.ds(0, 4)], x0_send.at[0], x0_recv.at[0], gx=above_x)
    x0_down = remote(C.at[pl.ds(4, 4)], C.at[pl.ds(CX + 4, 4)], x0_send.at[1], x0_recv.at[1], gx=below_x)
    pl.when(jnp.logical_not(last_x))(x0_up.start)
    pl.when(jnp.logical_not(first_x))(x0_down.start)
    lax.fori_loop(4, CX - 4, outer_y, 0, unroll=2)

    pl.when(jnp.logical_not(first_x))(x0_up.wait_recv)
    pl.when(jnp.logical_not(last_x))(x0_down.wait_recv)

    def finest_xz(i, carry):
        for t in range(4):
            rows = pl.ds(8 * t, 8)
            value = C[pl.ds(16 * i, 24), rows, :]
            moved = weighted([value[k : k + 16] for k in range(9)], w0)
            out[pl.ds(16 * i, 16), rows, :] = product(moved.reshape(128, CZ), W0[...]).reshape(16, 8, CZ)
        return carry

    lax.fori_loop(0, CX // 16, finest_xz, 0)

    pl.when(jnp.logical_not(first_y))(cy_up.wait_recv)
    pl.when(jnp.logical_not(last_y))(cy_down.wait_recv)
    pl.when(me_y >= 2)(c2_up.wait_recv)
    pl.when(me_y < across_y - 2)(c2_down.wait_recv)
    row8 = iota((8, CZ), 0)
    for level in (1, 2, 3):
        array, n, rows, count = B[level], NYL[level], ROWS[level], NXL[level] + 1
        wl = [taps[level, k] for k in range(2 * REACH + 1)]

        def along_y(x, carry, array=array, target=U[level], n=n, rows=rows, level=level, wl=wl):
            array[x, 4:12, :] = array[x, 4:12, :] + jnp.where(row8 < 5, YR[0, x], 0.0)
            array[x, 8 + n : 16 + n, :] = array[x, 8 + n : 16 + n, :] + jnp.where(row8 < 5, YR[1, x], 0.0)
            if level == 3:
                array[x, 4:5, :] = array[x, 4:5, :] + YR[0, x, 5:6, :]
                array[x, 16:17, :] = array[x, 16:17, :] + YR[1, x, 5:6, :]
            target[x] = weighted([array[x, 4 + k : 4 + k + rows, :] for k in range(9)], wl)
            return carry

        lax.fori_loop(0, count, along_y, 0)

        @pl.when(last_y)
        def _(target=U[level], n=n, count=count):
            target[:, n : n + 1, :] = jnp.zeros((count, 1, CZ), F32)

    others = pl.ds(0, across_x - 1)
    pltpu.make_async_copy(GB.at[others], GB.at[others], gb_recv).wait()
    row, col = iota((16, 16 * across_x), 0), iota((16, 16 * across_x), 1)
    spot, place = 8 * me_x + row, 8 * (col // 16) + col % 16
    valid = (row < 9) & (spot < 8 * across_x) & (col % 16 < 9) & (place < 8 * across_x)
    along = jnp.where(valid, gauss(spot - place, 8 * across_x), 0.0)
    value = jnp.dot(along, GB[...].reshape(16 * across_x, CZ), precision=HIGHEST, preferred_element_type=F32)
    keep = (lane8 // 8 == row8) & (lane8 < 24)
    spread = jnp.concatenate(
        [jnp.where(keep, jnp.broadcast_to(value[x : x + 1], (8, CZ)), 0.0) for x in range(9)], axis=0
    )
    r, c = iota((CZ, CZ), 0), iota((CZ, CZ), 1)
    pick = (c == 112 + r % 8).astype(F32)
    E4[:, 0:8, :] = jnp.dot(spread, pick, precision=HIGHEST, preferred_element_type=F32).reshape(9, 8, CZ)
    E4[:, 8:16, :] = jnp.zeros((9, 8, CZ), F32)

    for level, source, wide in ((3, E4, G3), (2, U3, G2), (1, U2, G1)):
        half = {3: 8, 2: 8, 1: 16}[level]
        target, rows, n = U[level], ROWS[level], NXL[level]
        first, cells = LANES[level]

        def widen(i, carry, source=source, wide=wide, half=half):
            low = source[i, pl.ds(0, half), :]
            wide[i, pl.ds(0, half, stride=2), :] = low
            if half == 8 and source is U3:
                high = pltpu.roll(low, 7, 0)
            elif half == 16:
                high = pltpu.roll(low, 15, 0)
            else:
                high = source[i, pl.ds(1, half), :]
            wide[i, pl.ds(1, half, stride=2), :] = 0.5 * (low + high)
            return carry

        lax.fori_loop(0, n // 2 + 1, widen, 0)
        lane = iota((rows, CZ), 1)
        own = (lane >= first) & (lane < first + cells)

        def climb(i, carry, target=target, wide=wide, rows=rows, own=own):
            low, high = wide[i, pl.ds(0, rows), :], wide[i + 1, pl.ds(0, rows), :]
            target[2 * i] = jnp.where(own, target[2 * i], low)
            target[2 * i + 1] = jnp.where(own, target[2 * i + 1], 0.5 * (low + high))
            return carry

        lax.fori_loop(0, n // 2, climb, 0)
        target[n] = jnp.where(own, target[n], wide[n // 2, pl.ds(0, rows), :])

    def rise_zy(i, carry):
        high, low = split(U1[pl.ds(i * 5, 5)].reshape(5 * 24, CZ))
        both = jnp.concatenate([high, low], axis=1)
        E1Z[pl.ds(i * 5, 5)] = jnp.dot(both, PZ[...], preferred_element_type=F32).reshape(5, 24, CZ)
        for j in range(5):
            x = i * 5 + j
            low, high = E1Z[x, 0:16, :], E1Z[x, 1:17, :]
            G0[x, pl.ds(0, 16, stride=2), :] = low
            G0[x, pl.ds(1, 16, stride=2), :] = 0.5 * (low + high)
        return carry

    lax.fori_loop(0, 13, rise_zy, 0)

    def finish(i, carry):
        low, high = G0[i], G0[i + 1]
        out[2 * i] = out[2 * i] + low
        out[2 * i + 1] = out[2 * i + 1] + 0.5 * (low + high)
        return carry

    lax.fori_loop(0, CX // 2, finish, 0)

    pl.when(jnp.logical_not(last_y))(y0_up.wait_send)
    pl.when(jnp.logical_not(first_y))(y0_down.wait_send)
    pl.when(jnp.logical_not(last_x))(x0_up.wait_send)
    pl.when(jnp.logical_not(first_x))(x0_down.wait_send)
    pl.when(jnp.logical_not(last_x))(cx_up.wait_send)
    pl.when(jnp.logical_not(first_x))(cx_down.wait_send)
    pl.when(jnp.logical_not(last_y))(cy_up.wait_send)
    pl.when(jnp.logical_not(first_y))(cy_down.wait_send)
    pl.when(me_y < across_y - 2)(c2_up.wait_send)
    pl.when(me_y >= 2)(c2_down.wait_send)
    others = pl.ds(0, across_y - 1)
    pltpu.make_async_copy(GA.at[others], GA.at[others], ga_send).wait()
    others = pl.ds(0, across_x - 1)
    pltpu.make_async_copy(GB.at[others], GB.at[others], gb_send).wait()


def solution(mesh):
    across_x, across_y = mesh.shape["gx"], mesh.shape["gy"]

    def vmem(*shape, dtype=F32):
        return pltpu.VMEM(shape, dtype)

    pair = pltpu.SemaphoreType.DMA((2,))
    single = pltpu.SemaphoreType.DMA
    scratch = [
        vmem(CX, 48, CZ),
        vmem(CX + 8, CY, CZ),
        vmem(65, 56, CZ), vmem(33, 40, CZ), vmem(17, 24, CZ), vmem(9, 24, CZ),
        vmem(73, 24, CZ), vmem(41, 16, CZ), vmem(25, 8, CZ), vmem(9, 8, CZ),
        vmem(65, 40, CZ), vmem(33, 32, CZ), vmem(17, 24, CZ),
        vmem(65, 24, CZ), vmem(33, 16, CZ), vmem(17, 8, CZ),
        vmem(9, 16, CZ), vmem(9, 16, CZ), vmem(17, 16, CZ), vmem(33, 32, CZ), vmem(65, 32, CZ),
        vmem(2, 5, 24, CZ), vmem(2, 5, 24, CZ),
        vmem(2, 65, 8, CZ), vmem(2, 65, 8, CZ),
        vmem(across_y, 8, CZ), vmem(across_x, 16, CZ),
        vmem(3 * CZ, CZ, dtype=BF16), vmem(3 * CZ, CZ, dtype=BF16), vmem(2 * CZ, CZ, dtype=BF16),
        vmem(65, 24, CZ),
        pltpu.SemaphoreType.DMA((4,)),
        pair, pair, pair, pair, pair, pair, pair, pair, pair, pair,
        single, single, single, single,
    ]

    def local(charge, level_taps):
        return pl.pallas_call(
            functools.partial(kernel, across_x, across_y),
            out_shape=jax.ShapeDtypeStruct((CX, CY, CZ), F32),
            in_specs=[pl.BlockSpec(memory_space=pltpu.SMEM), pl.BlockSpec(memory_space=pl.ANY)],
            out_specs=pl.BlockSpec(memory_space=pltpu.VMEM),
            scratch_shapes=scratch,
            compiler_params=pltpu.CompilerParams(
                collective_id=0, has_side_effects=True, vmem_limit_bytes=48 * 1024 * 1024
            ),
        )(level_taps, charge)

    spec = P("gx", "gy", None)
    return jax.shard_map(local, mesh=mesh, in_specs=(spec, P()), out_specs=spec, check_vma=False)
```

time: 488 us -> 37.6 us (0.08)
  the two profiles are of different devices: /device:TPU:195 before, /device:TPU:1 now
where the time goes in v1:
time: 37.6 us; the launch traced here: 37.5 us
  Pallas kernels  33.9 us (90%)
  local copies, waits for them, and re-layouts  3.59 us (10%)
    pallas_call x1, Pallas kernels, local(): pl.pallas_call(functools.partial(kernel, across_x, across_y), out_shape=j...  33.9 us
    unnamed x5, local copies, waits for them, and re-layouts  3.59 us

profile of v1, /device:TPU:1, one launch (start us, length us, event | category | flops | bytes accessed | tf_op | source)
XLA Modules:
  0.0 37.5 jit_solution(12757421559498689211)
XLA Ops:
  0.0 0.0 copy-start
  0.0 1.6 %copy-done = f32[128,32,128]{2,1,0:T(8,128)S(1)} copy-done((f32[128,32,128]{2,1,0:T(8,128)S(1)}, f32[128,32,128]{2,1,0:T(8,128)}, u32[]{:S(2)}) %copy-start) | copy-done | bytes 2097176
  1.6 0.0 copy-start.1
  1.6 0.7 %copy-done.1 = f32[4,9]{1,0:T(4,128)S(1)} copy-done((f32[4,9]{1,0:T(4,128)S(1)}, f32[4,9]{1,0:T(4,128)}, u32[]{:S(2)}) %copy-start.1) | copy-done | bytes 168
  2.3 33.9 %shard_map.28 = f32[128,32,128]{2,1,0:T(8,128)S(1)} custom-call(f32[4,9]{1,0:T(4,128)S(1)} %copy-done.1, f32[128,32,128]{2,1,0:T(8,128)S(1)} %copy-done), custom_call_target="tpu_custom_call" | custom-call | tf_op jit(solution)/shard_map/pallas_call | solution.py:514
  36.1 1.3 %copy.4 = f32[128,32,128]{2,1,0:T(8,128)} copy(f32[128,32,128]{2,1,0:T(8,128)S(1)} %shard_map.28) | data formatting | bytes 4194304
Async XLA Ops:
  0.0 1.6 %copy-start = (f32[128,32,128]{2,1,0:T(8,128)S(1)}, f32[128,32,128]{2,1,0:T(8,128)}, u32[]{:S(2)}) copy-start(f32[128,32,128]{2,1,0:T(8,128)} %q.1) | copy-start | bytes 6291460
  1.6 0.7 %copy-start.1 = (f32[4,9]{1,0:T(4,128)S(1)}, f32[4,9]{1,0:T(4,128)}, u32[]{:S(2)}) copy-start(f32[4,9]{1,0:T(4,128)} %taps.1) | copy-start | bytes 436

commit v2 on v1

--- a/solution.py
+++ b/solution.py
@@ -38,13 +38,15 @@
 
 def stacked(matrix):
     high, low = split(matrix)
-    return jnp.concatenate([high, high, low], axis=0)
+    upper = jnp.concatenate([high, low], axis=1)
+    lower = jnp.concatenate([high, jnp.zeros_like(high)], axis=1)
+    return jnp.concatenate([upper, lower], axis=0)
 
 
 def product(value, weights):
     high, low = split(value)
-    both = jnp.concatenate([high, low, high], axis=1)
-    return jnp.dot(both, weights, preferred_element_type=F32)
+    both = jnp.dot(jnp.concatenate([high, low], axis=1), weights, preferred_element_type=F32)
+    return both[:, :CZ] + both[:, CZ:]
 
 
 def toeplitz(taps, level, shape, offset):
@@ -91,10 +93,11 @@
 
 
 def kernel(
-    across_x, across_y, taps, q, out,
+    across_x, across_y, taps_in, q, out,
+    taps,
     E, C, T1, T2, T3, T4, A1, A2, A3, A4, B1, B2, B3, U1, U2, U3, E4, G3, G2, G1, G0,
     XS, XR, YS, YR, GA, GB, WZ, W0, PZ, E1Z,
-    in_sem, y0_send, y0_recv, x0_send, x0_recv, cx_send, cx_recv, cy_send, cy_recv,
+    taps_sem, in_sem, y0_send, y0_recv, x0_send, x0_recv, cx_send, cx_recv, cy_send, cy_recv,
     c2_send, c2_recv, ga_send, ga_recv, gb_send, gb_recv,
 ):
     me_x, me_y = lax.axis_index("gx"), lax.axis_index("gy")
@@ -102,6 +105,8 @@
     first_y, last_y = me_y == 0, me_y == across_y - 1
     A, B, U, T = {1: A1, 2: A2, 3: A3}, {1: B1, 2: B2, 3: B3}, {1: U1, 2: U2, 3: U3}, {2: T2, 3: T3, 4: T4}
 
+    few = pltpu.make_async_copy(taps_in, taps, taps_sem)
+    few.start()
     barrier = pltpu.get_barrier_semaphore()
 
     def greet_y(step, carry):
@@ -126,17 +131,15 @@
     for load in loads:
         load.start()
 
+    few.wait()
     WZ[...] = stacked(coarse_z(taps))
     W0[...] = stacked(toeplitz(taps, 0, (CZ, CZ), iota((CZ, CZ), 0) - iota((CZ, CZ), 1)))
     rise = prolong_z()
     PZ[...] = jnp.concatenate([rise, rise], axis=0)
 
     def blank(ref, count, *spans):
-        def body(i, carry):
-            for start, size in spans:
-                ref[i, pl.ds(start, size), :] = jnp.zeros((size, CZ), F32)
-            return carry
-        lax.fori_loop(0, count, body, 0)
+        for start, size in spans:
+            ref[:, start : start + size, :] = jnp.zeros((count, size, CZ), F32)
 
     blank(T1, 65, (0, 8), (40, 16))
     blank(T2, 33, (0, 8), (32, 8))
@@ -203,33 +206,31 @@
 
     lax.fori_loop(1, 64, down_x, 0, unroll=3)
 
-    def down_yz(i, carry):
-        at = pl.ds(i * 5, 5)
-        value = (
-            T1[at, pl.ds(7, 24, stride=2), :]
-            + 2.0 * T1[at, pl.ds(8, 24, stride=2), :]
-            + T1[at, pl.ds(9, 24, stride=2), :]
+    def down_y(i, carry):
+        E1Z[i] = (
+            T1[i, pl.ds(7, 24, stride=2), :] + 2.0 * T1[i, pl.ds(8, 24, stride=2), :] + T1[i, pl.ds(9, 24, stride=2), :]
         )
-        A1[pl.ds(4 + i * 5, 5)] = product(value.reshape(5 * 24, CZ), WZ[...]).reshape(5, 24, CZ)
-        return carry
-
-    lax.fori_loop(0, 13, down_yz, 0)
+        return carry
+
+    lax.fori_loop(0, 65, down_y, 0, unroll=5)
+
+    A1[4:69] = product(E1Z[...].reshape(66 * 24, CZ), WZ[...]).reshape(66, 24, CZ)[0:65]
 
     for level in (2, 3, 4):
         finer, mid = A[level - 1], T[level]
         coarser, shift = (A[level], 4) if level < 4 else (A4, 0)
         inner, rows = ROWS[level - 1], ROWS[level]
 
-        def down(i, carry, finer=finer, mid=mid, coarser=coarser, shift=shift, inner=inner, rows=rows):
-            mid[i, pl.ds(8, inner), :] = finer[2 * i + 3] + 2.0 * finer[2 * i + 4] + finer[2 * i + 5]
-            coarser[i + shift] = (
-                mid[i, pl.ds(7, rows, stride=2), :]
-                + 2.0 * mid[i, pl.ds(8, rows, stride=2), :]
-                + mid[i, pl.ds(9, rows, stride=2), :]
-            )
-            return carry
-
-        lax.fori_loop(0, NXL[level] + 1, down, 0)
+        n = NXL[level]
+        pairs = finer[4 : 2 * n + 4].reshape(n, 2, inner, CZ)
+        even, odd = pairs[:, 0], pairs[:, 1]
+        mid[0:n, 8 : 8 + inner, :] = 2.0 * even + odd + finer[3 : 2 * n + 3].reshape(n, 2, inner, CZ)[:, 0]
+        mid[n, 8 : 8 + inner, :] = finer[2 * n + 3] + 2.0 * finer[2 * n + 4]
+        coarser[shift : shift + n + 1] = (
+            mid[:, pl.ds(7, rows, stride=2), :]
+            + 2.0 * mid[:, pl.ds(8, rows, stride=2), :]
+            + mid[:, pl.ds(9, rows, stride=2), :]
+        )
 
     lane8 = iota((8, CZ), 1)
     message = jnp.zeros((8, CZ), F32)
@@ -286,7 +287,7 @@
             target[i, pl.ds(8, rows), :] = weighted([array[i + k] for k in range(9)], wl)
             return carry
 
-        lax.fori_loop(0, n + 1, along_x, 0)
+        lax.fori_loop(0, n + 1, along_x, 0, unroll={1: 5, 2: 3, 3: 1}[level])
 
         @pl.when(last_x)
         def _(target=B[level], rows=rows, n=n):
@@ -296,19 +297,12 @@
         def _(target=B[level], level=level, n=n):
             target[:, pl.ds(8 + NYL[level], 1), :] = jnp.zeros((n + 1, 1, CZ), F32)
 
-    def pack(x, levels):
-        for way in (0, 1):
-            lane = iota((8, CZ), 1)
-            value = None
-            for level in levels:
-                start = 8 + (NYL[level] - 4 if way == 0 else 0)
-                piece = B[level][x, pl.ds(start, 8), :]
-                value = piece if value is None else jnp.where(lane >= LANES[level][0], piece, value)
-            YS[way, x] = value
-
-    lax.fori_loop(0, 17, lambda x, c: (pack(x, (1, 2, 3)), c)[1], 0)
-    lax.fori_loop(17, 33, lambda x, c: (pack(x, (1, 2)), c)[1], 0)
-    lax.fori_loop(33, 65, lambda x, c: (pack(x, (1,)), c)[1], 0)
+    lane = iota((8, CZ), 1)
+    for way in (0, 1):
+        start = {level: 8 + (NYL[level] - 4 if way == 0 else 0) for level in (1, 2, 3)}
+        YS[way] = B1[:, start[1] : start[1] + 8, :]
+        YS[way, 0:33] = jnp.where(lane >= 64, B2[:, start[2] : start[2] + 8, :], B1[0:33, start[1] : start[1] + 8, :])
+        YS[way, 0:17] = jnp.where(lane >= 96, B3[:, start[3] : start[3] + 8, :], YS[way, 0:17])
     rows5 = pl.ds(0, 5)
     cy_up = remote(YS.at[0, :, rows5], YR.at[0, :, rows5], cy_send.at[0], cy_recv.at[0], gy=above_y)
     cy_down = remote(YS.at[1, :, rows5], YR.at[1, :, rows5], cy_send.at[1], cy_recv.at[1], gy=below_y)
@@ -367,15 +361,17 @@
     pl.when(jnp.logical_not(first_x))(x0_up.wait_recv)
     pl.when(jnp.logical_not(last_x))(x0_down.wait_recv)
 
-    def finest_xz(i, carry):
+    def finest_x(i, carry):
+        w0 = [taps[0, k] for k in range(2 * REACH + 1)]
         for t in range(4):
             rows = pl.ds(8 * t, 8)
             value = C[pl.ds(16 * i, 24), rows, :]
-            moved = weighted([value[k : k + 16] for k in range(9)], w0)
-            out[pl.ds(16 * i, 16), rows, :] = product(moved.reshape(128, CZ), W0[...]).reshape(16, 8, CZ)
-        return carry
-
-    lax.fori_loop(0, CX // 16, finest_xz, 0)
+            out[pl.ds(16 * i, 16), rows, :] = weighted([value[k : k + 16] for k in range(9)], w0)
+        return carry
+
+    lax.fori_loop(0, CX // 16, finest_x, 0)
+
+    out[...] = product(out[...].reshape(CX * CY, CZ), W0[...]).reshape(CX, CY, CZ)
 
     pl.when(jnp.logical_not(first_y))(cy_up.wait_recv)
     pl.when(jnp.logical_not(last_y))(cy_down.wait_recv)
@@ -395,11 +391,11 @@
             target[x] = weighted([array[x, 4 + k : 4 + k + rows, :] for k in range(9)], wl)
             return carry
 
-        lax.fori_loop(0, count, along_y, 0)
+        lax.fori_loop(0, count, along_y, 0, unroll={1: 5, 2: 3, 3: 1}[level])
 
         @pl.when(last_y)
         def _(target=U[level], n=n, count=count):
-            target[:, n : n + 1, :] = jnp.zeros((count, 1, CZ), F32)
+            target[0:count, n : n + 1, :] = jnp.zeros((count, 1, CZ), F32)
 
     others = pl.ds(0, across_x - 1)
     pltpu.make_async_copy(GB.at[others], GB.at[others], gb_recv).wait()
@@ -422,43 +418,31 @@
         target, rows, n = U[level], ROWS[level], NXL[level]
         first, cells = LANES[level]
 
-        def widen(i, carry, source=source, wide=wide, half=half):
-            low = source[i, pl.ds(0, half), :]
-            wide[i, pl.ds(0, half, stride=2), :] = low
-            if half == 8 and source is U3:
-                high = pltpu.roll(low, 7, 0)
-            elif half == 16:
-                high = pltpu.roll(low, 15, 0)
-            else:
-                high = source[i, pl.ds(1, half), :]
-            wide[i, pl.ds(1, half, stride=2), :] = 0.5 * (low + high)
-            return carry
-
-        lax.fori_loop(0, n // 2 + 1, widen, 0)
+        low = source[:, 0:half, :]
+        if half == source.shape[1]:
+            high = pltpu.roll(low, half - 1, 1)
+        else:
+            high = source[:, 1 : half + 1, :]
+        wide[:, pl.ds(0, half, stride=2), :] = low
+        wide[:, pl.ds(1, half, stride=2), :] = 0.5 * (low + high)
         lane = iota((rows, CZ), 1)
         own = (lane >= first) & (lane < first + cells)
-
-        def climb(i, carry, target=target, wide=wide, rows=rows, own=own):
-            low, high = wide[i, pl.ds(0, rows), :], wide[i + 1, pl.ds(0, rows), :]
-            target[2 * i] = jnp.where(own, target[2 * i], low)
-            target[2 * i + 1] = jnp.where(own, target[2 * i + 1], 0.5 * (low + high))
-            return carry
-
-        lax.fori_loop(0, n // 2, climb, 0)
-        target[n] = jnp.where(own, target[n], wide[n // 2, pl.ds(0, rows), :])
-
-    def rise_zy(i, carry):
-        high, low = split(U1[pl.ds(i * 5, 5)].reshape(5 * 24, CZ))
-        both = jnp.concatenate([high, low], axis=1)
-        E1Z[pl.ds(i * 5, 5)] = jnp.dot(both, PZ[...], preferred_element_type=F32).reshape(5, 24, CZ)
-        for j in range(5):
-            x = i * 5 + j
-            low, high = E1Z[x, 0:16, :], E1Z[x, 1:17, :]
-            G0[x, pl.ds(0, 16, stride=2), :] = low
-            G0[x, pl.ds(1, 16, stride=2), :] = 0.5 * (low + high)
-        return carry
-
-    lax.fori_loop(0, 13, rise_zy, 0)
+        low, high = wide[0 : n // 2, 0:rows, :], wide[1 : n // 2 + 1, 0:rows, :]
+        both = jnp.stack([low, 0.5 * (low + high)], axis=1).reshape(n, rows, CZ)
+        target[0:n] = jnp.where(own, target[0:n], both)
+        target[n] = jnp.where(own, target[n], wide[n // 2, 0:rows, :])
+
+    high, low = split(U1[...].reshape(66 * 24, CZ))
+    both = jnp.concatenate([high, low], axis=1)
+    E1Z[...] = jnp.dot(both, PZ[...], preferred_element_type=F32).reshape(66, 24, CZ)
+
+    def rise_y(x, carry):
+        low, high = E1Z[x, 0:16, :], E1Z[x, 1:17, :]
+        G0[x, pl.ds(0, 16, stride=2), :] = low
+        G0[x, pl.ds(1, 16, stride=2), :] = 0.5 * (low + high)
+        return carry
+
+    lax.fori_loop(0, 65, rise_y, 0, unroll=5)
 
     def finish(i, carry):
         low, high = G0[i], G0[i + 1]
@@ -466,7 +450,7 @@
         out[2 * i + 1] = out[2 * i + 1] + 0.5 * (low + high)
         return carry
 
-    lax.fori_loop(0, CX // 2, finish, 0)
+    lax.fori_loop(0, CX // 2, finish, 0, unroll=2)
 
     pl.when(jnp.logical_not(last_y))(y0_up.wait_send)
     pl.when(jnp.logical_not(first_y))(y0_down.wait_send)
@@ -493,19 +477,20 @@
     pair = pltpu.SemaphoreType.DMA((2,))
     single = pltpu.SemaphoreType.DMA
     scratch = [
+        pltpu.SMEM((4, 9), F32),
         vmem(CX, 48, CZ),
         vmem(CX + 8, CY, CZ),
         vmem(65, 56, CZ), vmem(33, 40, CZ), vmem(17, 24, CZ), vmem(9, 24, CZ),
         vmem(73, 24, CZ), vmem(41, 16, CZ), vmem(25, 8, CZ), vmem(9, 8, CZ),
         vmem(65, 40, CZ), vmem(33, 32, CZ), vmem(17, 24, CZ),
-        vmem(65, 24, CZ), vmem(33, 16, CZ), vmem(17, 8, CZ),
+        vmem(66, 24, CZ), vmem(33, 16, CZ), vmem(17, 8, CZ),
         vmem(9, 16, CZ), vmem(9, 16, CZ), vmem(17, 16, CZ), vmem(33, 32, CZ), vmem(65, 32, CZ),
         vmem(2, 5, 24, CZ), vmem(2, 5, 24, CZ),
         vmem(2, 65, 8, CZ), vmem(2, 65, 8, CZ),
         vmem(across_y, 8, CZ), vmem(across_x, 16, CZ),
-        vmem(3 * CZ, CZ, dtype=BF16), vmem(3 * CZ, CZ, dtype=BF16), vmem(2 * CZ, CZ, dtype=BF16),
-        vmem(65, 24, CZ),
-        pltpu.SemaphoreType.DMA((4,)),
+        vmem(2 * CZ, 2 * CZ, dtype=BF16), vmem(2 * CZ, 2 * CZ, dtype=BF16), vmem(2 * CZ, CZ, dtype=BF16),
+        vmem(66, 24, CZ),
+        single, pltpu.SemaphoreType.DMA((4,)),
         pair, pair, pair, pair, pair, pair, pair, pair, pair, pair,
         single, single, single, single,
     ]
@@ -514,13 +499,13 @@
         return pl.pallas_call(
             functools.partial(kernel, across_x, across_y),
             out_shape=jax.ShapeDtypeStruct((CX, CY, CZ), F32),
-            in_specs=[pl.BlockSpec(memory_space=pltpu.SMEM), pl.BlockSpec(memory_space=pl.ANY)],
+            in_specs=[pl.BlockSpec(memory_space=pltpu.HBM), pl.BlockSpec(memory_space=pltpu.HBM)],
             out_specs=pl.BlockSpec(memory_space=pltpu.VMEM),
             scratch_shapes=scratch,
             compiler_params=pltpu.CompilerParams(
                 collective_id=0, has_side_effects=True, vmem_limit_bytes=48 * 1024 * 1024
             ),
-        )(level_taps, charge)
+        )(*(pltpu.with_memory_space_constraint(array, pltpu.HBM) for array in (level_taps, charge)))
 
     spec = P("gx", "gy", None)
     return jax.shard_map(local, mesh=mesh, in_specs=(spec, P()), out_specs=spec, check_vma=False)

time: 37.6 us -> 30.4 us (0.81)
  Pallas kernels: 33.9 us -> 28.9 us
  local copies, waits for them, and re-layouts: 3.59 us -> 1.32 us
    pallas_call x1, Pallas kernels: 33.9 us -> 28.9 us  [local(): pl.pallas_call(functools.partial(kernel, across_x, across_y), out_shape=j...]
    unnamed x5 -> x1, local copies, waits for them, and re-layouts: 3.59 us -> 1.32 us
where the time goes in v2:
time: 30.4 us; the launch traced here: 30.3 us
  Pallas kernels  28.9 us (95%)
  local copies, waits for them, and re-layouts  1.32 us (4%)
    pallas_call x1, Pallas kernels, local(): pl.pallas_call(functools.partial(kernel, across_x, across_y), out_shape=j...  28.9 us
    unnamed x1, local copies, waits for them, and re-layouts  1.32 us

profile of v2, /device:TPU:1, one launch (start us, length us, event | category | flops | bytes accessed | tf_op | source)
XLA Modules:
  0.0 30.3 jit_solution(4590324008516390365)
XLA Ops:
  0.0 28.9 %shard_map.28 = f32[128,32,128]{2,1,0:T(8,128)S(1)} custom-call(f32[4,9]{1,0:T(4,128)} %taps_in.1, f32[128,32,128]{2,1,0:T(8,128)} %q.1), custom_call_target="tpu_custom_call" | custom-call | tf_op jit(solution)/shard_map/pallas_call | solution.py:499
  28.9 1.3 %copy.4 = f32[128,32,128]{2,1,0:T(8,128)} copy(f32[128,32,128]{2,1,0:T(8,128)S(1)} %shard_map.28) | data formatting | bytes 4194304

commit v3 on v2

--- a/solution.py
+++ b/solution.py
@@ -93,12 +93,12 @@
 
 
 def kernel(
-    across_x, across_y, taps_in, q, out,
+    across_x, across_y, taps_in, q, out, coarsest, slopes,
     taps,
-    E, C, T1, T2, T3, T4, A1, A2, A3, A4, B1, B2, B3, U1, U2, U3, E4, G3, G2, G1, G0,
-    XS, XR, YS, YR, GA, GB, WZ, W0, PZ, E1Z,
+    E, C, T1, T2, T3, T4, A1, A2, A3, A4, B1, B2, B3, U1, U2, U3, G2, G1, G0,
+    XS, XR, YS, YR, GA, GB, WZ, W0, PZ, P4, E1Z,
     taps_sem, in_sem, y0_send, y0_recv, x0_send, x0_recv, cx_send, cx_recv, cy_send, cy_recv,
-    c2_send, c2_recv, ga_send, ga_recv, gb_send, gb_recv,
+    c2_send, c2_recv, ga_send, ga_recv, gc_send, gc_recv, gb_send, gb_recv,
 ):
     me_x, me_y = lax.axis_index("gx"), lax.axis_index("gy")
     first_x, last_x = me_x == 0, me_x == across_x - 1
@@ -109,16 +109,18 @@
     few.start()
     barrier = pltpu.get_barrier_semaphore()
 
-    def greet_y(step, carry):
-        pl.semaphore_signal(barrier, inc=1, device_id={"gy": lax.rem(me_y + step, across_y)}, device_id_type=MESH)
-        return carry
-
-    def greet_x(step, carry):
-        pl.semaphore_signal(barrier, inc=1, device_id={"gx": lax.rem(me_x + step, across_x)}, device_id_type=MESH)
-        return carry
-
-    lax.fori_loop(1, across_y, greet_y, 0)
-    lax.fori_loop(1, across_x, greet_x, 0)
+    group = min(8, across_y)
+    groups = across_y // group
+    rank, base = lax.rem(me_y, group), me_y - lax.rem(me_y, group)
+    mates = [base + lax.rem(rank + s, group) for s in range(1, group)]
+    peers = [lax.rem(me_y + group * s, across_y) for s in range(1, groups)]
+    columns = [lax.rem(me_x + s, across_x) for s in range(1, across_x)]
+    steps = (1, 2, across_y - 2, across_y - 1) if across_y > 4 else ()
+    around = [lax.rem(me_y + s, across_y) for s in steps]
+    for y in around + mates + peers:
+        pl.semaphore_signal(barrier, inc=1, device_id={"gy": y}, device_id_type=MESH)
+    for x in columns:
+        pl.semaphore_signal(barrier, inc=1, device_id={"gx": x}, device_id_type=MESH)
 
     parts = 4
     depth = CX // parts
@@ -131,12 +133,6 @@
     for load in loads:
         load.start()
 
-    few.wait()
-    WZ[...] = stacked(coarse_z(taps))
-    W0[...] = stacked(toeplitz(taps, 0, (CZ, CZ), iota((CZ, CZ), 0) - iota((CZ, CZ), 1)))
-    rise = prolong_z()
-    PZ[...] = jnp.concatenate([rise, rise], axis=0)
-
     def blank(ref, count, *spans):
         for start, size in spans:
             ref[:, start : start + size, :] = jnp.zeros((count, size, CZ), F32)
@@ -179,13 +175,24 @@
         C[CX + 4 : CX + 8] = jnp.zeros((4, CY, CZ), F32)
         XR[1] = jnp.zeros((5, 24, CZ), F32)
 
-    pl.semaphore_wait(barrier, across_x + across_y - 2)
+    rise = prolong_z()
+    PZ[...] = jnp.concatenate([rise, rise], axis=0)
+    r, a = iota((CZ, CZ), 0), iota((CZ, CZ), 1)
+    rise = jnp.maximum(0, 16 - jnp.abs(a - 16 * (r % 8))).astype(F32) / 16.0
+    rise = jnp.where(r < 24, rise, 0.0).astype(BF16)
+    P4[...] = jnp.concatenate([rise, rise], axis=0)
+
+    pl.semaphore_wait(barrier, len(around + mates + peers + columns))
 
     def remote(src, dst, send, recv, **target):
         return pltpu.make_async_remote_copy(
             src_ref=src, dst_ref=dst, send_sem=send, recv_sem=recv, device_id=target, device_id_type=MESH
         )
 
+    def drain(ref, count, sem):
+        if count:
+            pltpu.make_async_copy(ref.at[pl.ds(0, count)], ref.at[pl.ds(0, count)], sem).wait()
+
     above_y, below_y = lax.rem(me_y + 1, across_y), lax.rem(me_y + across_y - 1, across_y)
     above_x, below_x = lax.rem(me_x + 1, across_x), lax.rem(me_x + across_x - 1, across_x)
 
@@ -214,6 +221,9 @@
 
     lax.fori_loop(0, 65, down_y, 0, unroll=5)
 
+    few.wait()
+    WZ[...] = stacked(coarse_z(taps))
+    W0[...] = stacked(toeplitz(taps, 0, (CZ, CZ), iota((CZ, CZ), 0) - iota((CZ, CZ), 1)))
     A1[4:69] = product(E1Z[...].reshape(66 * 24, CZ), WZ[...]).reshape(66, 24, CZ)[0:65]
 
     for level in (2, 3, 4):
@@ -238,12 +248,8 @@
         value = jnp.where((lane8 >= 112) & (lane8 < 120), A4[x], 0.0)
         message = message + pltpu.roll(value, (8 * x - 112) % CZ, 1)
     GA[me_y] = message
-
-    def send_a(step, carry):
-        remote(GA.at[me_y], GA.at[me_y], ga_send, ga_recv, gy=lax.rem(me_y + step, across_y)).start()
-        return carry
-
-    lax.fori_loop(1, across_y, send_a, 0)
+    for y in mates:
+        remote(GA.at[me_y], GA.at[me_y], ga_send, ga_recv, gy=y).start()
 
     @pl.when(last_x)
     def _():
@@ -272,6 +278,27 @@
         return carry
 
     lax.fori_loop(0, CX, mid_y, 0, unroll=2)
+
+    pl.when(jnp.logical_not(first_y))(y0_up.wait_recv)
+    pl.when(jnp.logical_not(last_y))(y0_down.wait_recv)
+
+    def outer_y(i, carry):
+        C[4 + i, 0:8, :] = weighted([E[i, 4 + k : 12 + k, :] for k in range(9)], w0)
+        C[4 + i, 24:32, :] = weighted([E[i, 28 + k : 36 + k, :] for k in range(9)], w0)
+        return carry
+
+    lax.fori_loop(0, 4, outer_y, 0, unroll=2)
+    lax.fori_loop(CX - 4, CX, outer_y, 0, unroll=2)
+    x0_up = remote(C.at[pl.ds(CX, 4)], C.at[pl.ds(0, 4)], x0_send.at[0], x0_recv.at[0], gx=above_x)
+    x0_down = remote(C.at[pl.ds(4, 4)], C.at[pl.ds(CX + 4, 4)], x0_send.at[1], x0_recv.at[1], gx=below_x)
+    pl.when(jnp.logical_not(last_x))(x0_up.start)
+    pl.when(jnp.logical_not(first_x))(x0_down.start)
+
+    lax.fori_loop(4, CX - 4, outer_y, 0, unroll=2)
+
+    drain(GA, group - 1, ga_recv)
+    for y in peers:
+        remote(GA.at[pl.ds(base, group)], GA.at[pl.ds(base, group)], gc_send, gc_recv, gy=y).start()
 
     pl.when(jnp.logical_not(first_x))(cx_up.wait_recv)
     pl.when(jnp.logical_not(last_x))(cx_down.wait_recv)
@@ -320,8 +347,22 @@
     pl.when(me_y < across_y - 2)(c2_up.start)
     pl.when(me_y >= 2)(c2_down.start)
 
-    others = pl.ds(0, across_y - 1)
-    pltpu.make_async_copy(GA.at[others], GA.at[others], ga_recv).wait()
+    pl.when(jnp.logical_not(first_x))(x0_up.wait_recv)
+    pl.when(jnp.logical_not(last_x))(x0_down.wait_recv)
+
+    def finest_x(i, carry):
+        w0 = [taps[0, k] for k in range(2 * REACH + 1)]
+        for t in range(4):
+            rows = pl.ds(8 * t, 8)
+            value = C[pl.ds(16 * i, 24), rows, :]
+            out[pl.ds(16 * i, 16), rows, :] = weighted([value[k : k + 16] for k in range(9)], w0)
+        return carry
+
+    lax.fori_loop(0, CX // 16, finest_x, 0)
+
+    out[...] = product(out[...].reshape(CX * CY, CZ), W0[...]).reshape(CX, CY, CZ)
+
+    drain(GA, (groups - 1) * group, gc_recv)
     row, col = iota((8, 8 * across_y), 0), iota((8, 8 * across_y), 1)
     spot, place = 2 * me_y + row, 2 * (col // 8) + col % 8
     valid = (row < 3) & (spot < 2 * across_y) & (col % 8 < 3) & (place < 2 * across_y)
@@ -335,43 +376,8 @@
     r, c = iota((3 * CZ, CZ), 0), iota((3 * CZ, CZ), 1)
     pick = (c == 8 * (r // CZ) + r % 8).astype(F32)
     GB[me_x] = jnp.dot(spread, pick, precision=HIGHEST, preferred_element_type=F32)
-
-    def send_b(step, carry):
-        remote(GB.at[me_x], GB.at[me_x], gb_send, gb_recv, gx=lax.rem(me_x + step, across_x)).start()
-        return carry
-
-    lax.fori_loop(1, across_x, send_b, 0)
-
-    pl.when(jnp.logical_not(first_y))(y0_up.wait_recv)
-    pl.when(jnp.logical_not(last_y))(y0_down.wait_recv)
-
-    def outer_y(i, carry):
-        C[4 + i, 0:8, :] = weighted([E[i, 4 + k : 12 + k, :] for k in range(9)], w0)
-        C[4 + i, 24:32, :] = weighted([E[i, 28 + k : 36 + k, :] for k in range(9)], w0)
-        return carry
-
-    lax.fori_loop(0, 4, outer_y, 0)
-    lax.fori_loop(CX - 4, CX, outer_y, 0)
-    x0_up = remote(C.at[pl.ds(CX, 4)], C.at[pl.ds(0, 4)], x0_send.at[0], x0_recv.at[0], gx=above_x)
-    x0_down = remote(C.at[pl.ds(4, 4)], C.at[pl.ds(CX + 4, 4)], x0_send.at[1], x0_recv.at[1], gx=below_x)
-    pl.when(jnp.logical_not(last_x))(x0_up.start)
-    pl.when(jnp.logical_not(first_x))(x0_down.start)
-    lax.fori_loop(4, CX - 4, outer_y, 0, unroll=2)
-
-    pl.when(jnp.logical_not(first_x))(x0_up.wait_recv)
-    pl.when(jnp.logical_not(last_x))(x0_down.wait_recv)
-
-    def finest_x(i, carry):
-        w0 = [taps[0, k] for k in range(2 * REACH + 1)]
-        for t in range(4):
-            rows = pl.ds(8 * t, 8)
-            value = C[pl.ds(16 * i, 24), rows, :]
-            out[pl.ds(16 * i, 16), rows, :] = weighted([value[k : k + 16] for k in range(9)], w0)
-        return carry
-
-    lax.fori_loop(0, CX // 16, finest_x, 0)
-
-    out[...] = product(out[...].reshape(CX * CY, CZ), W0[...]).reshape(CX, CY, CZ)
+    for x in columns:
+        remote(GB.at[me_x], GB.at[me_x], gb_send, gb_recv, gx=x).start()
 
     pl.when(jnp.logical_not(first_y))(cy_up.wait_recv)
     pl.when(jnp.logical_not(last_y))(cy_down.wait_recv)
@@ -397,32 +403,15 @@
         def _(target=U[level], n=n, count=count):
             target[0:count, n : n + 1, :] = jnp.zeros((count, 1, CZ), F32)
 
-    others = pl.ds(0, across_x - 1)
-    pltpu.make_async_copy(GB.at[others], GB.at[others], gb_recv).wait()
-    row, col = iota((16, 16 * across_x), 0), iota((16, 16 * across_x), 1)
-    spot, place = 8 * me_x + row, 8 * (col // 16) + col % 16
-    valid = (row < 9) & (spot < 8 * across_x) & (col % 16 < 9) & (place < 8 * across_x)
-    along = jnp.where(valid, gauss(spot - place, 8 * across_x), 0.0)
-    value = jnp.dot(along, GB[...].reshape(16 * across_x, CZ), precision=HIGHEST, preferred_element_type=F32)
-    keep = (lane8 // 8 == row8) & (lane8 < 24)
-    spread = jnp.concatenate(
-        [jnp.where(keep, jnp.broadcast_to(value[x : x + 1], (8, CZ)), 0.0) for x in range(9)], axis=0
-    )
-    r, c = iota((CZ, CZ), 0), iota((CZ, CZ), 1)
-    pick = (c == 112 + r % 8).astype(F32)
-    E4[:, 0:8, :] = jnp.dot(spread, pick, precision=HIGHEST, preferred_element_type=F32).reshape(9, 8, CZ)
-    E4[:, 8:16, :] = jnp.zeros((9, 8, CZ), F32)
-
-    for level, source, wide in ((3, E4, G3), (2, U3, G2), (1, U2, G1)):
-        half = {3: 8, 2: 8, 1: 16}[level]
+    lane = iota((8, CZ), 1)
+    U3[...] = jnp.where((lane >= 96) & (lane < 112), U3[...], 0.0)
+    for level, source, wide in ((2, U3, G2), (1, U2, G1)):
+        half = {2: 8, 1: 16}[level]
         target, rows, n = U[level], ROWS[level], NXL[level]
         first, cells = LANES[level]
 
         low = source[:, 0:half, :]
-        if half == source.shape[1]:
-            high = pltpu.roll(low, half - 1, 1)
-        else:
-            high = source[:, 1 : half + 1, :]
+        high = pltpu.roll(low, half - 1, 1)
         wide[:, pl.ds(0, half, stride=2), :] = low
         wide[:, pl.ds(1, half, stride=2), :] = 0.5 * (low + high)
         lane = iota((rows, CZ), 1)
@@ -451,6 +440,22 @@
         return carry
 
     lax.fori_loop(0, CX // 2, finish, 0, unroll=2)
+
+    drain(GB, across_x - 1, gb_recv)
+    row, col = iota((16, 16 * across_x), 0), iota((16, 16 * across_x), 1)
+    spot, place = 8 * me_x + row, 8 * (col // 16) + col % 16
+    valid = (row < 9) & (spot < 8 * across_x) & (col % 16 < 9) & (place < 8 * across_x)
+    along = jnp.where(valid, gauss(spot - place, 8 * across_x), 0.0)
+    value = jnp.dot(along, GB[...].reshape(16 * across_x, CZ), precision=HIGHEST, preferred_element_type=F32)
+    y, lane = iota((CY, CZ), 0), iota((CY, CZ), 1)
+    share = jnp.maximum(0, 16 - jnp.abs(y - 16 * (lane // 8))).astype(F32) / 16.0
+    share = jnp.where(lane < 24, share, 0.0)
+    spread = jnp.concatenate([share * value[x : x + 1] for x in range(9)], axis=0)
+    high, low = split(spread)
+    both = jnp.concatenate([high, low], axis=1)
+    value = jnp.dot(both, P4[...], preferred_element_type=F32).reshape(9, CY, CZ)
+    coarsest[...] = value[:8]
+    slopes[...] = (value[1:] - value[:8]) * (1.0 / 16.0)
 
     pl.when(jnp.logical_not(last_y))(y0_up.wait_send)
     pl.when(jnp.logical_not(first_y))(y0_down.wait_send)
@@ -462,10 +467,9 @@
     pl.when(jnp.logical_not(first_y))(cy_down.wait_send)
     pl.when(me_y < across_y - 2)(c2_up.wait_send)
     pl.when(me_y >= 2)(c2_down.wait_send)
-    others = pl.ds(0, across_y - 1)
-    pltpu.make_async_copy(GA.at[others], GA.at[others], ga_send).wait()
-    others = pl.ds(0, across_x - 1)
-    pltpu.make_async_copy(GB.at[others], GB.at[others], gb_send).wait()
+    drain(GA, group - 1, ga_send)
+    drain(GA, (groups - 1) * group, gc_send)
+    drain(GB, across_x - 1, gb_send)
 
 
 def solution(mesh):
@@ -484,28 +488,31 @@
         vmem(73, 24, CZ), vmem(41, 16, CZ), vmem(25, 8, CZ), vmem(9, 8, CZ),
         vmem(65, 40, CZ), vmem(33, 32, CZ), vmem(17, 24, CZ),
         vmem(66, 24, CZ), vmem(33, 16, CZ), vmem(17, 8, CZ),
-        vmem(9, 16, CZ), vmem(9, 16, CZ), vmem(17, 16, CZ), vmem(33, 32, CZ), vmem(65, 32, CZ),
+        vmem(17, 16, CZ), vmem(33, 32, CZ), vmem(65, 32, CZ),
         vmem(2, 5, 24, CZ), vmem(2, 5, 24, CZ),
         vmem(2, 65, 8, CZ), vmem(2, 65, 8, CZ),
         vmem(across_y, 8, CZ), vmem(across_x, 16, CZ),
-        vmem(2 * CZ, 2 * CZ, dtype=BF16), vmem(2 * CZ, 2 * CZ, dtype=BF16), vmem(2 * CZ, CZ, dtype=BF16),
+        vmem(2 * CZ, 2 * CZ, dtype=BF16), vmem(2 * CZ, 2 * CZ, dtype=BF16), vmem(2 * CZ, CZ, dtype=BF16), vmem(2 * CZ, CZ, dtype=BF16),
         vmem(66, 24, CZ),
         single, pltpu.SemaphoreType.DMA((4,)),
         pair, pair, pair, pair, pair, pair, pair, pair, pair, pair,
-        single, single, single, single,
+        single, single, single, single, single, single,
     ]
 
     def local(charge, level_taps):
-        return pl.pallas_call(
+        fine, coarse, slope = pl.pallas_call(
             functools.partial(kernel, across_x, across_y),
-            out_shape=jax.ShapeDtypeStruct((CX, CY, CZ), F32),
+            out_shape=[jax.ShapeDtypeStruct((CX, CY, CZ), F32), *[jax.ShapeDtypeStruct((8, CY, CZ), F32)] * 2],
             in_specs=[pl.BlockSpec(memory_space=pltpu.HBM), pl.BlockSpec(memory_space=pltpu.HBM)],
-            out_specs=pl.BlockSpec(memory_space=pltpu.VMEM),
+            out_specs=[pl.BlockSpec(memory_space=pltpu.VMEM)] * 3,
             scratch_shapes=scratch,
             compiler_params=pltpu.CompilerParams(
                 collective_id=0, has_side_effects=True, vmem_limit_bytes=48 * 1024 * 1024
             ),
         )(*(pltpu.with_memory_space_constraint(array, pltpu.HBM) for array in (level_taps, charge)))
+        step = lax.broadcasted_iota(F32, (8, 16, CY, CZ), 1)
+        rise = coarse[:, None] + step * slope[:, None]
+        return (fine.reshape(8, 16, CY, CZ) + rise).reshape(CX, CY, CZ)
 
     spec = P("gx", "gy", None)
     return jax.shard_map(local, mesh=mesh, in_specs=(spec, P()), out_specs=spec, check_vma=False)

time: 30.4 us -> 28.4 us (0.934)
  the two profiles are of different devices: /device:TPU:1 before, /device:TPU:6 now
where the time goes in v3:
time: 28.4 us; the launch traced here: 28.3 us
  Pallas kernels  26.6 us (94%)
  other arithmetic  1.63 us (6%)
    pallas_call x1, Pallas kernels, local(): pl.pallas_call(functools.partial(kernel, across_x, across_y), out_shape=[...  26.6 us
    add x1, other arithmetic, local(): return (fine.reshape(8, 16, CY, CZ) + rise).reshape(CX, CY, CZ)  1.63 us

profile of v3, /device:TPU:6, one launch (start us, length us, event | category | flops | bytes accessed | tf_op | source)
XLA Modules:
  0.0 28.3 jit_solution(13370619028258949519)
XLA Ops:
  0.0 0.1 iota.12
  0.1 26.6 %shard_map.28 = (f32[128,32,128]{2,1,0:T(8,128)S(1)}, f32[8,32,128]{2,1,0:T(8,128)S(1)}, f32[8,32,128]{2,1,0:T(8,128)S(1)}) custom-call(f32[4,9]{1,0:T(4,128)} %taps_in.1, f32[128,32,128]{2,1,0:T(8,128)} %q.1), custom_call_target="tpu_custom_call" | custom-call | tf_op jit(solution)/shard_map/pallas_call | solution.py:503
  26.7 1.6 %fusion.1 = f32[128,32,128]{2,1,0:T(8,128)} fusion(f32[128,32,128]{2,1,0:T(8,128)S(1)} %get-tuple-element.8, f32[8,32,128]{2,1,0:T(8,128)S(1)} %get-tuple-element.10, f32[128]{0:T(128)S(1)} %iota.12, f32[8,32,128]{2,1,0:T(8,128)S(1)} %get-tuple-element.9), kind=kLoop, calls=%fused_computation.2 | loop fusion | flops 1572864 | bytes 4456960 | tf_op jit(solution)/shard_map/add | solution.py:515
  (1 shorter events, 0.0 us)

commit v4 on v3

--- a/solution.py
+++ b/solution.py
@@ -15,7 +15,7 @@
 
 CX, CY, CZ = 128, 32, 128
 REACH = 4
-LANES = {1: (0, 64), 2: (64, 32), 3: (96, 16), 4: (112, 8)}
+LANES = {1: (0, 64), 2: (64, 32), 3: (96, 16)}
 NXL = {1: 64, 2: 32, 3: 16, 4: 8}
 NYL = {1: 16, 2: 8, 3: 4, 4: 2}
 ROWS = {1: 24, 2: 16, 3: 8, 4: 8}
@@ -66,10 +66,7 @@
         weight = jnp.maximum(0, step - jnp.abs(a - step * (c - first)))
         down = jnp.where(here, weight.astype(F32) * 2.0 ** (-5 * level), down)
         inside = here & (a >= first) & (a < first + cells)
-        if level < 4:
-            block = toeplitz(taps, level, (CZ, CZ), a - c)
-        else:
-            block = gauss(a - c, cells)
+        block = toeplitz(taps, level, (CZ, CZ), a - c)
         mix = jnp.where(inside, block, mix)
     return jnp.dot(down, mix, precision=HIGHEST, preferred_element_type=F32)
 
@@ -95,33 +92,18 @@
 def kernel(
     across_x, across_y, taps_in, q, out, coarsest, slopes,
     taps,
-    E, C, T1, T2, T3, T4, A1, A2, A3, A4, B1, B2, B3, U1, U2, U3, G2, G1, G0,
-    XS, XR, YS, YR, GA, GB, WZ, W0, PZ, P4, E1Z,
+    E, C, T1, T2, T3, T4, R1, R2, R3, A1, A2, A3, B1, B2, B3, U1, U2, U3, G2, G1, G0,
+    XS, XR, YS, YR, GA, GB, WZ, W0, PZ, P4, Z4, E1Z,
     taps_sem, in_sem, y0_send, y0_recv, x0_send, x0_recv, cx_send, cx_recv, cy_send, cy_recv,
-    c2_send, c2_recv, ga_send, ga_recv, gc_send, gc_recv, gb_send, gb_recv,
+    c2_send, c2_recv, ga_send, ga_recv, gb_send, gb_recv,
 ):
     me_x, me_y = lax.axis_index("gx"), lax.axis_index("gy")
     first_x, last_x = me_x == 0, me_x == across_x - 1
     first_y, last_y = me_y == 0, me_y == across_y - 1
-    A, B, U, T = {1: A1, 2: A2, 3: A3}, {1: B1, 2: B2, 3: B3}, {1: U1, 2: U2, 3: U3}, {2: T2, 3: T3, 4: T4}
+    R, A, B, U, T = {1: R1, 2: R2, 3: R3}, {1: A1, 2: A2, 3: A3}, {1: B1, 2: B2, 3: B3}, {1: U1, 2: U2, 3: U3}, {2: T2, 3: T3, 4: T4}
 
     few = pltpu.make_async_copy(taps_in, taps, taps_sem)
     few.start()
-    barrier = pltpu.get_barrier_semaphore()
-
-    group = min(8, across_y)
-    groups = across_y // group
-    rank, base = lax.rem(me_y, group), me_y - lax.rem(me_y, group)
-    mates = [base + lax.rem(rank + s, group) for s in range(1, group)]
-    peers = [lax.rem(me_y + group * s, across_y) for s in range(1, groups)]
-    columns = [lax.rem(me_x + s, across_x) for s in range(1, across_x)]
-    steps = (1, 2, across_y - 2, across_y - 1) if across_y > 4 else ()
-    around = [lax.rem(me_y + s, across_y) for s in steps]
-    for y in around + mates + peers:
-        pl.semaphore_signal(barrier, inc=1, device_id={"gy": y}, device_id_type=MESH)
-    for x in columns:
-        pl.semaphore_signal(barrier, inc=1, device_id={"gx": x}, device_id_type=MESH)
-
     parts = 4
     depth = CX // parts
     loads = [
@@ -133,6 +115,21 @@
     for load in loads:
         load.start()
 
+    cores = 2 if across_y > 1 else 1
+    chips = across_y // cores
+    core = lax.rem(me_y, cores)
+    near_by = [
+        (lax.rem(me_x + x, across_x), me_y - core + lax.rem(core + c, cores))
+        for x in range(across_x) for c in range(cores) if x or c
+    ]
+    far_off = [(me_x, lax.rem(me_y + cores * step, across_y)) for step in range(1, chips)]
+    steps = (1, 2, across_y - 2, across_y - 1) if across_y > 4 else ()
+    around = [(me_x, lax.rem(me_y + step, across_y)) for step in steps]
+    barrier = pltpu.get_barrier_semaphore()
+    for x, y in around + near_by + far_off:
+        pl.semaphore_signal(barrier, inc=1, device_id=(x, y), device_id_type=MESH)
+
+
     def blank(ref, count, *spans):
         for start, size in spans:
             ref[:, start : start + size, :] = jnp.zeros((count, size, CZ), F32)
@@ -144,8 +141,9 @@
     for level in (1, 2, 3):
         blank(B[level], NXL[level] + 1, (0, 8), *(((16, 8),) if level == 3 else ()))
         rows = ROWS[level]
-        A[level][0:4] = jnp.zeros((4, rows, CZ), F32)
-        A[level][NXL[level] + 5 : NXL[level] + 9] = jnp.zeros((4, rows, CZ), F32)
+        R[level][0] = jnp.zeros((rows, CZ), F32)
+    GA[:, 2:8, :] = jnp.zeros((across_x * cores, 6, CZ), F32)
+    GB[:, 6:8, :] = jnp.zeros((chips, 2, CZ), F32)
 
     @pl.when(first_y)
     def _():
@@ -175,81 +173,89 @@
         C[CX + 4 : CX + 8] = jnp.zeros((4, CY, CZ), F32)
         XR[1] = jnp.zeros((5, 24, CZ), F32)
 
+    a, c = iota((CZ, CZ), 0), iota((CZ, CZ), 1)
+    weight = jnp.maximum(0, 16 - jnp.abs(a - 16 * c)).astype(F32) * 2.0**-20
+    weight = jnp.where(c < 8, weight, 0.0)
+    block = jnp.where(a < 8, gauss(a - c % 8, 8), 0.0)
+    Z4[...] = jnp.dot(weight, block, precision=HIGHEST, preferred_element_type=F32)
     rise = prolong_z()
     PZ[...] = jnp.concatenate([rise, rise], axis=0)
     r, a = iota((CZ, CZ), 0), iota((CZ, CZ), 1)
     rise = jnp.maximum(0, 16 - jnp.abs(a - 16 * (r % 8))).astype(F32) / 16.0
-    rise = jnp.where(r < 24, rise, 0.0).astype(BF16)
+    rise = jnp.where(r < 72, rise, 0.0).astype(BF16)
     P4[...] = jnp.concatenate([rise, rise], axis=0)
 
-    pl.semaphore_wait(barrier, len(around + mates + peers + columns))
 
     def remote(src, dst, send, recv, **target):
         return pltpu.make_async_remote_copy(
             src_ref=src, dst_ref=dst, send_sem=send, recv_sem=recv, device_id=target, device_id_type=MESH
         )
 
-    def drain(ref, count, sem):
+    def drain(ref, count, rows, sem):
         if count:
-            pltpu.make_async_copy(ref.at[pl.ds(0, count)], ref.at[pl.ds(0, count)], sem).wait()
+            part = ref.at[pl.ds(0, count), pl.ds(0, rows)]
+            pltpu.make_async_copy(part, part, sem).wait()
 
     above_y, below_y = lax.rem(me_y + 1, across_y), lax.rem(me_y + across_y - 1, across_y)
     above_x, below_x = lax.rem(me_x + 1, across_x), lax.rem(me_x + across_x - 1, across_x)
 
     y0_up = remote(q.at[:, pl.ds(CY - 4, 4)], E.at[:, pl.ds(4, 4)], y0_send.at[0], y0_recv.at[0], gy=above_y)
     y0_down = remote(q.at[:, pl.ds(0, 4)], E.at[:, pl.ds(40, 4)], y0_send.at[1], y0_recv.at[1], gy=below_y)
+    for load in loads:
+        load.wait()
+
+    T1[0, 8:40, :] = 2.0 * E[0, 8:40, :] + E[1, 8:40, :]
+    T1[64, 8:40, :] = E[CX - 1, 8:40, :]
+
+    def down_x(i, carry):
+        T1[i, 8:40, :] = E[2 * i - 1, 8:40, :] + 2.0 * E[2 * i, 8:40, :] + E[2 * i + 1, 8:40, :]
+        return carry
+
+    lax.fori_loop(1, 64, down_x, 0, unroll=3)
+
+    def down_y(i, carry):
+        R1[i + 1] = (
+            T1[i, pl.ds(7, 24, stride=2), :] + 2.0 * T1[i, pl.ds(8, 24, stride=2), :] + T1[i, pl.ds(9, 24, stride=2), :]
+        )
+        return carry
+
+    lax.fori_loop(0, 65, down_y, 0, unroll=5)
+
+    pl.semaphore_wait(barrier, len(around + near_by + far_off))
     pl.when(jnp.logical_not(last_y))(y0_up.start)
     pl.when(jnp.logical_not(first_y))(y0_down.start)
-
-    for load in loads:
-        load.wait()
-
-    T1[0, 8:40, :] = 2.0 * E[0, 8:40, :] + E[1, 8:40, :]
-    T1[64, 8:40, :] = E[CX - 1, 8:40, :]
-
-    def down_x(i, carry):
-        T1[i, 8:40, :] = E[2 * i - 1, 8:40, :] + 2.0 * E[2 * i, 8:40, :] + E[2 * i + 1, 8:40, :]
-        return carry
-
-    lax.fori_loop(1, 64, down_x, 0, unroll=3)
-
-    def down_y(i, carry):
-        E1Z[i] = (
-            T1[i, pl.ds(7, 24, stride=2), :] + 2.0 * T1[i, pl.ds(8, 24, stride=2), :] + T1[i, pl.ds(9, 24, stride=2), :]
-        )
-        return carry
-
-    lax.fori_loop(0, 65, down_y, 0, unroll=5)
-
-    few.wait()
-    WZ[...] = stacked(coarse_z(taps))
-    W0[...] = stacked(toeplitz(taps, 0, (CZ, CZ), iota((CZ, CZ), 0) - iota((CZ, CZ), 1)))
-    A1[4:69] = product(E1Z[...].reshape(66 * 24, CZ), WZ[...]).reshape(66, 24, CZ)[0:65]
-
     for level in (2, 3, 4):
-        finer, mid = A[level - 1], T[level]
-        coarser, shift = (A[level], 4) if level < 4 else (A4, 0)
+        finer, mid, n = R[level - 1], T[level], NXL[level]
         inner, rows = ROWS[level - 1], ROWS[level]
-
-        n = NXL[level]
-        pairs = finer[4 : 2 * n + 4].reshape(n, 2, inner, CZ)
-        even, odd = pairs[:, 0], pairs[:, 1]
-        mid[0:n, 8 : 8 + inner, :] = 2.0 * even + odd + finer[3 : 2 * n + 3].reshape(n, 2, inner, CZ)[:, 0]
-        mid[n, 8 : 8 + inner, :] = finer[2 * n + 3] + 2.0 * finer[2 * n + 4]
-        coarser[shift : shift + n + 1] = (
+        pairs = finer[1 : 2 * n + 1].reshape(n, 2, inner, CZ)
+        before = finer[0 : 2 * n].reshape(n, 2, inner, CZ)
+        mid[0:n, 8 : 8 + inner, :] = before[:, 0] + 2.0 * pairs[:, 0] + pairs[:, 1]
+        mid[n, 8 : 8 + inner, :] = finer[2 * n] + 2.0 * finer[2 * n + 1]
+        value = (
             mid[:, pl.ds(7, rows, stride=2), :]
             + 2.0 * mid[:, pl.ds(8, rows, stride=2), :]
             + mid[:, pl.ds(9, rows, stride=2), :]
         )
-
-    lane8 = iota((8, CZ), 1)
-    message = jnp.zeros((8, CZ), F32)
-    for x in range(9):
-        value = jnp.where((lane8 >= 112) & (lane8 < 120), A4[x], 0.0)
-        message = message + pltpu.roll(value, (8 * x - 112) % CZ, 1)
-    GA[me_y] = message
-    for y in mates:
-        remote(GA.at[me_y], GA.at[me_y], ga_send, ga_recv, gy=y).start()
+        if level < 4:
+            R[level][1 : n + 2] = value
+
+    value = jnp.dot(value.reshape(72, CZ), Z4[...], precision=HIGHEST, preferred_element_type=F32)
+    row, lane = iota((72, CZ), 0), iota((72, CZ), 1)
+    value = jnp.where((lane // 8 == 3 * (row // 16) + row % 8) & (row % 8 < 3), value, 0.0)
+    pick = ((iota((8, 72), 1) // 8) % 2 == iota((8, 72), 0)).astype(F32)
+    mine = me_x * cores + core
+    GA[mine, 0:2, :] = jnp.dot(pick, value, precision=HIGHEST, preferred_element_type=F32)[0:2]
+    two = pl.ds(0, 2)
+    for x, y in near_by:
+        remote(GA.at[mine, two], GA.at[mine, two], ga_send, ga_recv, gx=x, gy=y).start()
+
+
+    few.wait()
+    WZ[...] = stacked(coarse_z(taps))
+    W0[...] = stacked(toeplitz(taps, 0, (CZ, CZ), iota((CZ, CZ), 0) - iota((CZ, CZ), 1)))
+    A1[4:69] = product(R1[1:67].reshape(66 * 24, CZ), WZ[...]).reshape(66, 24, CZ)[0:65]
+    A2[4:37] = product(R2[1:34].reshape(33 * 16, CZ), WZ[...]).reshape(33, 16, CZ)
+    A3[4:21] = product(R3[1:19].reshape(18 * 8, CZ), WZ[...]).reshape(18, 8, CZ)[0:17]
 
     @pl.when(last_x)
     def _():
@@ -278,27 +284,6 @@
         return carry
 
     lax.fori_loop(0, CX, mid_y, 0, unroll=2)
-
-    pl.when(jnp.logical_not(first_y))(y0_up.wait_recv)
-    pl.when(jnp.logical_not(last_y))(y0_down.wait_recv)
-
-    def outer_y(i, carry):
-        C[4 + i, 0:8, :] = weighted([E[i, 4 + k : 12 + k, :] for k in range(9)], w0)
-        C[4 + i, 24:32, :] = weighted([E[i, 28 + k : 36 + k, :] for k in range(9)], w0)
-        return carry
-
-    lax.fori_loop(0, 4, outer_y, 0, unroll=2)
-    lax.fori_loop(CX - 4, CX, outer_y, 0, unroll=2)
-    x0_up = remote(C.at[pl.ds(CX, 4)], C.at[pl.ds(0, 4)], x0_send.at[0], x0_recv.at[0], gx=above_x)
-    x0_down = remote(C.at[pl.ds(4, 4)], C.at[pl.ds(CX + 4, 4)], x0_send.at[1], x0_recv.at[1], gx=below_x)
-    pl.when(jnp.logical_not(last_x))(x0_up.start)
-    pl.when(jnp.logical_not(first_x))(x0_down.start)
-
-    lax.fori_loop(4, CX - 4, outer_y, 0, unroll=2)
-
-    drain(GA, group - 1, ga_recv)
-    for y in peers:
-        remote(GA.at[pl.ds(base, group)], GA.at[pl.ds(base, group)], gc_send, gc_recv, gy=y).start()
 
     pl.when(jnp.logical_not(first_x))(cx_up.wait_recv)
     pl.when(jnp.logical_not(last_x))(cx_down.wait_recv)
@@ -347,6 +332,50 @@
     pl.when(me_y < across_y - 2)(c2_up.start)
     pl.when(me_y >= 2)(c2_down.start)
 
+    pl.when(jnp.logical_not(first_y))(y0_up.wait_recv)
+    pl.when(jnp.logical_not(last_y))(y0_down.wait_recv)
+
+    def outer_y(i, carry):
+        C[4 + i, 0:8, :] = weighted([E[i, 4 + k : 12 + k, :] for k in range(9)], w0)
+        C[4 + i, 24:32, :] = weighted([E[i, 28 + k : 36 + k, :] for k in range(9)], w0)
+        return carry
+
+    lax.fori_loop(0, 4, outer_y, 0, unroll=2)
+    lax.fori_loop(CX - 4, CX, outer_y, 0, unroll=2)
+    x0_up = remote(C.at[pl.ds(CX, 4)], C.at[pl.ds(0, 4)], x0_send.at[0], x0_recv.at[0], gx=above_x)
+    x0_down = remote(C.at[pl.ds(4, 4)], C.at[pl.ds(CX + 4, 4)], x0_send.at[1], x0_recv.at[1], gx=below_x)
+    pl.when(jnp.logical_not(last_x))(x0_up.start)
+    pl.when(jnp.logical_not(first_x))(x0_down.start)
+
+    lax.fori_loop(4, CX - 4, outer_y, 0, unroll=2)
+
+    row, col = iota((cores * 80, 8 * across_x * cores), 0), iota((cores * 80, 8 * across_x * cores), 1)
+    cell, slot = 2 * ((row // 16) % 5) + col % 8, col // 8
+    spot, place = 8 * me_x + row % 16, 8 * (slot // cores) + cell
+    valid = (slot % cores == row // 80) & (col % 8 < 2) & (cell < 9) & (place < 8 * across_x)
+    valid = valid & (row % 16 < 9) & (spot < 8 * across_x)
+    along = jnp.where(valid, gauss(spot - place, 8 * across_x), 0.0)
+    r, c = iota((CZ, 3 * CZ), 0), iota((CZ, 3 * CZ), 1)
+    pick = (r == 8 * (c // CZ) + c % 8).astype(F32)
+    row, col = iota((8, 48 * cores), 0), iota((8, 48 * cores), 1)
+    gather = ((row // 3 == (col // 16) % cores) & (row % 3 == col // (16 * cores))).astype(F32)
+    drain(GA, across_x * cores - 1, 2, ga_recv)
+    value = jnp.dot(along, GA[...].reshape(8 * across_x * cores, CZ), precision=HIGHEST, preferred_element_type=F32)
+    value = value.reshape(cores, 5, 16, CZ)
+    lane = iota((cores, 16, CZ), 2)
+    total = jnp.where(lane < 24, value[:, 0], 0.0)
+    for g in range(1, 5):
+        total = total + jnp.where(lane < 24, pltpu.roll(value[:, g], CZ - 24 * g, 2), 0.0)
+    value = jnp.dot(total.reshape(cores * 16, CZ), pick, precision=HIGHEST, preferred_element_type=F32)
+    row, lane = iota((cores * 16, CZ), 0), iota((cores * 16, CZ), 1)
+    keep = (lane // 8 == row % 16) & (lane < 72)
+    value = jnp.concatenate([jnp.where(keep, value[:, y * CZ : y * CZ + CZ], 0.0) for y in range(3)], axis=0)
+    here = me_y // cores
+    GB[here] = jnp.dot(gather, value, precision=HIGHEST, preferred_element_type=F32)
+    six = pl.ds(0, 6)
+    for x, y in far_off:
+        remote(GB.at[here, six], GB.at[here, six], gb_send, gb_recv, gy=y).start()
+
     pl.when(jnp.logical_not(first_x))(x0_up.wait_recv)
     pl.when(jnp.logical_not(last_x))(x0_down.wait_recv)
 
@@ -361,23 +390,6 @@
     lax.fori_loop(0, CX // 16, finest_x, 0)
 
     out[...] = product(out[...].reshape(CX * CY, CZ), W0[...]).reshape(CX, CY, CZ)
-
-    drain(GA, (groups - 1) * group, gc_recv)
-    row, col = iota((8, 8 * across_y), 0), iota((8, 8 * across_y), 1)
-    spot, place = 2 * me_y + row, 2 * (col // 8) + col % 8
-    valid = (row < 3) & (spot < 2 * across_y) & (col % 8 < 3) & (place < 2 * across_y)
-    along = jnp.where(valid, gauss(spot - place, 2 * across_y), 0.0)
-    value = jnp.dot(along, GA[...].reshape(8 * across_y, CZ), precision=HIGHEST, preferred_element_type=F32)
-    lane16, row16 = iota((16, CZ), 1), iota((16, CZ), 0)
-    keep = (lane16 // 8 == row16) & (row16 < 9)
-    spread = jnp.concatenate(
-        [jnp.where(keep, jnp.broadcast_to(value[y : y + 1], (16, CZ)), 0.0) for y in range(3)], axis=1
-    )
-    r, c = iota((3 * CZ, CZ), 0), iota((3 * CZ, CZ), 1)
-    pick = (c == 8 * (r // CZ) + r % 8).astype(F32)
-    GB[me_x] = jnp.dot(spread, pick, precision=HIGHEST, preferred_element_type=F32)
-    for x in columns:
-        remote(GB.at[me_x], GB.at[me_x], gb_send, gb_recv, gx=x).start()
 
     pl.when(jnp.logical_not(first_y))(cy_up.wait_recv)
     pl.when(jnp.logical_not(last_y))(cy_down.wait_recv)
@@ -441,16 +453,19 @@
 
     lax.fori_loop(0, CX // 2, finish, 0, unroll=2)
 
-    drain(GB, across_x - 1, gb_recv)
-    row, col = iota((16, 16 * across_x), 0), iota((16, 16 * across_x), 1)
-    spot, place = 8 * me_x + row, 8 * (col // 16) + col % 16
-    valid = (row < 9) & (spot < 8 * across_x) & (col % 16 < 9) & (place < 8 * across_x)
-    along = jnp.where(valid, gauss(spot - place, 8 * across_x), 0.0)
-    value = jnp.dot(along, GB[...].reshape(16 * across_x, CZ), precision=HIGHEST, preferred_element_type=F32)
-    y, lane = iota((CY, CZ), 0), iota((CY, CZ), 1)
-    share = jnp.maximum(0, 16 - jnp.abs(y - 16 * (lane // 8))).astype(F32) / 16.0
-    share = jnp.where(lane < 24, share, 0.0)
-    spread = jnp.concatenate([share * value[x : x + 1] for x in range(9)], axis=0)
+    row, col = iota((CY, 8 * chips), 0), iota((CY, 8 * chips), 1)
+    place = 2 * (cores * (col // 8) + (col % 8) // 3) + (col % 8) % 3
+    valid = (col % 8 < 3 * cores) & (place < 2 * across_y)
+    along = jnp.zeros((CY, 8 * chips), F32)
+    for y in range(3):
+        spot = 2 * me_y + y
+        share = jnp.maximum(0, 16 - jnp.abs(row - 16 * y)).astype(F32) / 16.0
+        term = jnp.where(valid & (spot < 2 * across_y), gauss(spot - place, 2 * across_y), 0.0)
+        along = along + share * term
+    drain(GB, chips - 1, 6, gb_recv)
+    value = jnp.dot(along, GB[...].reshape(8 * chips, CZ), precision=HIGHEST, preferred_element_type=F32)
+    lane = iota((CY, CZ), 1)
+    spread = jnp.concatenate([jnp.where(lane // 8 == x, value, 0.0) for x in range(9)], axis=0)
     high, low = split(spread)
     both = jnp.concatenate([high, low], axis=1)
     value = jnp.dot(both, P4[...], preferred_element_type=F32).reshape(9, CY, CZ)
@@ -467,13 +482,28 @@
     pl.when(jnp.logical_not(first_y))(cy_down.wait_send)
     pl.when(me_y < across_y - 2)(c2_up.wait_send)
     pl.when(me_y >= 2)(c2_down.wait_send)
-    drain(GA, group - 1, ga_send)
-    drain(GA, (groups - 1) * group, gc_send)
-    drain(GB, across_x - 1, gb_send)
+    drain(GA, across_x * cores - 1, 2, ga_send)
+    drain(GB, chips - 1, 6, gb_send)
+
+
+def last(fine, coarse, slope, out, done, sem):
+    chunks = 8
+    depth = CX // chunks
+    copies = []
+    for i in range(chunks):
+        for x in range(i * depth, i * depth + depth):
+            done[x] = fine[x] + (coarse[x // 16] + float(x % 16) * slope[x // 16])
+        at = pl.ds(i * depth, depth)
+        copies.append(pltpu.make_async_copy(done.at[at], out.at[at], sem.at[i]))
+        copies[-1].start()
+    for copy in copies:
+        copy.wait()
 
 
 def solution(mesh):
     across_x, across_y = mesh.shape["gx"], mesh.shape["gy"]
+
+    cores = 2 if across_y > 1 else 1
 
     def vmem(*shape, dtype=F32):
         return pltpu.VMEM(shape, dtype)
@@ -485,18 +515,19 @@
         vmem(CX, 48, CZ),
         vmem(CX + 8, CY, CZ),
         vmem(65, 56, CZ), vmem(33, 40, CZ), vmem(17, 24, CZ), vmem(9, 24, CZ),
-        vmem(73, 24, CZ), vmem(41, 16, CZ), vmem(25, 8, CZ), vmem(9, 8, CZ),
+        vmem(67, 24, CZ), vmem(35, 16, CZ), vmem(19, 8, CZ),
+        vmem(73, 24, CZ), vmem(41, 16, CZ), vmem(25, 8, CZ),
         vmem(65, 40, CZ), vmem(33, 32, CZ), vmem(17, 24, CZ),
         vmem(66, 24, CZ), vmem(33, 16, CZ), vmem(17, 8, CZ),
         vmem(17, 16, CZ), vmem(33, 32, CZ), vmem(65, 32, CZ),
         vmem(2, 5, 24, CZ), vmem(2, 5, 24, CZ),
         vmem(2, 65, 8, CZ), vmem(2, 65, 8, CZ),
-        vmem(across_y, 8, CZ), vmem(across_x, 16, CZ),
+        vmem(across_x * cores, 8, CZ), vmem(across_y // cores, 8, CZ),
         vmem(2 * CZ, 2 * CZ, dtype=BF16), vmem(2 * CZ, 2 * CZ, dtype=BF16), vmem(2 * CZ, CZ, dtype=BF16), vmem(2 * CZ, CZ, dtype=BF16),
-        vmem(66, 24, CZ),
+        vmem(CZ, CZ), vmem(66, 24, CZ),
         single, pltpu.SemaphoreType.DMA((4,)),
         pair, pair, pair, pair, pair, pair, pair, pair, pair, pair,
-        single, single, single, single, single, single,
+        single, single, single, single,
     ]
 
     def local(charge, level_taps):
@@ -510,9 +541,14 @@
                 collective_id=0, has_side_effects=True, vmem_limit_bytes=48 * 1024 * 1024
             ),
         )(*(pltpu.with_memory_space_constraint(array, pltpu.HBM) for array in (level_taps, charge)))
-        step = lax.broadcasted_iota(F32, (8, 16, CY, CZ), 1)
-        rise = coarse[:, None] + step * slope[:, None]
-        return (fine.reshape(8, 16, CY, CZ) + rise).reshape(CX, CY, CZ)
+        return pl.pallas_call(
+            last,
+            out_shape=jax.ShapeDtypeStruct((CX, CY, CZ), F32),
+            in_specs=[pl.BlockSpec(memory_space=pltpu.VMEM)] * 3,
+            out_specs=pl.BlockSpec(memory_space=pltpu.HBM),
+            scratch_shapes=[vmem(CX, CY, CZ), pltpu.SemaphoreType.DMA((8,))],
+            compiler_params=pltpu.CompilerParams(vmem_limit_bytes=8 * 1024 * 1024),
+        )(fine, coarse, slope)
 
     spec = P("gx", "gy", None)
     return jax.shard_map(local, mesh=mesh, in_specs=(spec, P()), out_specs=spec, check_vma=False)

time: 28.4 us -> 24.7 us (0.87)
  the two profiles are of different devices: /device:TPU:6 before, /device:TPU:1 now
where the time goes in v4:
time: 24.7 us; the launch traced here: 24.5 us
  Pallas kernels  24.5 us (99%)
    pallas_call x1, Pallas kernels, local(): pl.pallas_call(functools.partial(kernel, across_x, across_y), out_shape=[...  23.1 us
    pallas_call x1, Pallas kernels, local(): pl.pallas_call(last, out_shape=jax.ShapeDtypeStruct((CX, CY, CZ), F32), i...  1.4 us

profile of v4, /device:TPU:1, one launch (start us, length us, event | category | flops | bytes accessed | tf_op | source)
XLA Modules:
  0.0 24.5 jit_solution(9618185915309595348)
XLA Ops:
  0.0 23.1 %shard_map.28 = (f32[128,32,128]{2,1,0:T(8,128)S(1)}, f32[8,32,128]{2,1,0:T(8,128)S(1)}, f32[8,32,128]{2,1,0:T(8,128)S(1)}) custom-call(f32[4,9]{1,0:T(4,128)} %taps_in.1, f32[128,32,128]{2,1,0:T(8,128)} %q.1), custom_call_target="tpu_custom_call" | custom-call | tf_op jit(solution)/shard_map/pallas_call | solution.py:534
  23.1 1.4 %shard_map.29 = f32[128,32,128]{2,1,0:T(8,128)} custom-call(f32[128,32,128]{2,1,0:T(8,128)S(1)} %get-tuple-element.8.fine, f32[8,32,128]{2,1,0:T(8,128)S(1)} %get-tuple-element.9.coarse, f32[8,32,128]{2,1,0:T(8,128)S(1)} %get-tuple-element.10.slope), custom_call_target="tpu_custom_call" | custom-call | tf_op jit(solution)/shard_map/pallas_call | solution.py:544

commit v5 on v4

--- a/solution.py
+++ b/solution.py
@@ -47,6 +47,18 @@
     high, low = split(value)
     both = jnp.dot(jnp.concatenate([high, low], axis=1), weights, preferred_element_type=F32)
     return both[:, :CZ] + both[:, CZ:]
+
+
+def picked(matrix, value):
+    both = jnp.concatenate(split(value), axis=0)
+    return jnp.dot(jnp.concatenate([matrix.astype(BF16)] * 2, axis=1), both, preferred_element_type=F32)
+
+
+def general(matrix, value):
+    (m_high, m_low), (v_high, v_low) = split(matrix), split(value)
+    left = jnp.concatenate([m_high, m_low, m_high], axis=1)
+    right = jnp.concatenate([v_high, v_high, v_low], axis=0)
+    return jnp.dot(left, right, preferred_element_type=F32)
 
 
 def toeplitz(taps, level, shape, offset):
@@ -92,28 +104,24 @@
 def kernel(
     across_x, across_y, taps_in, q, out, coarsest, slopes,
     taps,
-    E, C, T1, T2, T3, T4, R1, R2, R3, A1, A2, A3, B1, B2, B3, U1, U2, U3, G2, G1, G0,
-    XS, XR, YS, YR, GA, GB, WZ, W0, PZ, P4, Z4, E1Z,
+    E, C, T1, T2, T3, X4, R1, R2, R3, A1, A2, A3, B1, B2, B3, U1, U2, U3, G2, G1, G0,
+    XS, XR, YS, YR, GA, GB, WZ, W0, PZ, P4, Z4, K4, GX, PX, GY, E1Z,
     taps_sem, in_sem, y0_send, y0_recv, x0_send, x0_recv, cx_send, cx_recv, cy_send, cy_recv,
     c2_send, c2_recv, ga_send, ga_recv, gb_send, gb_recv,
 ):
     me_x, me_y = lax.axis_index("gx"), lax.axis_index("gy")
     first_x, last_x = me_x == 0, me_x == across_x - 1
     first_y, last_y = me_y == 0, me_y == across_y - 1
-    R, A, B, U, T = {1: R1, 2: R2, 3: R3}, {1: A1, 2: A2, 3: A3}, {1: B1, 2: B2, 3: B3}, {1: U1, 2: U2, 3: U3}, {2: T2, 3: T3, 4: T4}
+    R, A, B, U, T = {1: R1, 2: R2, 3: R3}, {1: A1, 2: A2, 3: A3}, {1: B1, 2: B2, 3: B3}, {1: U1, 2: U2, 3: U3}, {2: T2, 3: T3}
 
     few = pltpu.make_async_copy(taps_in, taps, taps_sem)
     few.start()
-    parts = 4
-    depth = CX // parts
-    loads = [
-        pltpu.make_async_copy(
-            q.at[pl.ds(i * depth, depth)], E.at[pl.ds(i * depth, depth), pl.ds(8, CY)], in_sem.at[i]
-        )
-        for i in range(parts)
-    ]
-    for load in loads:
-        load.start()
+    def load(i):
+        at = pl.ds(i * 16, 16)
+        return pltpu.make_async_copy(q.at[at], E.at[at, pl.ds(8, CY)], in_sem.at[i])
+
+    for i in range(CX // 16):
+        load(i).start()
 
     cores = 2 if across_y > 1 else 1
     chips = across_y // cores
@@ -137,7 +145,7 @@
     blank(T1, 65, (0, 8), (40, 16))
     blank(T2, 33, (0, 8), (32, 8))
     blank(T3, 17, (0, 8))
-    blank(T4, 9, (0, 8), (16, 8))
+    X4[0] = jnp.zeros((CY, CZ), F32)
     for level in (1, 2, 3):
         blank(B[level], NXL[level] + 1, (0, 8), *(((16, 8),) if level == 3 else ()))
         rows = ROWS[level]
@@ -177,14 +185,37 @@
     weight = jnp.maximum(0, 16 - jnp.abs(a - 16 * c)).astype(F32) * 2.0**-20
     weight = jnp.where(c < 8, weight, 0.0)
     block = jnp.where(a < 8, gauss(a - c % 8, 8), 0.0)
-    Z4[...] = jnp.dot(weight, block, precision=HIGHEST, preferred_element_type=F32)
+    Z4[...] = stacked(jnp.dot(weight, block, precision=HIGHEST, preferred_element_type=F32))
+    row, lane = iota((9 * CY, CZ), 0), iota((9 * CY, CZ), 1)
+    weight = jnp.maximum(0, 16 - jnp.abs(row % CY - 16 * ((lane // 8) % 3))).astype(F32)
+    K4[...] = jnp.where(lane // 24 == row // (2 * CY), weight, 0.0)
     rise = prolong_z()
     PZ[...] = jnp.concatenate([rise, rise], axis=0)
     r, a = iota((CZ, CZ), 0), iota((CZ, CZ), 1)
     rise = jnp.maximum(0, 16 - jnp.abs(a - 16 * (r % 8))).astype(F32) / 16.0
     rise = jnp.where(r < 72, rise, 0.0).astype(BF16)
     P4[...] = jnp.concatenate([rise, rise], axis=0)
-
+    row, col = iota((cores * 80, 8 * across_x * cores), 0), iota((cores * 80, 8 * across_x * cores), 1)
+    cell, slot = 2 * ((row // 16) % 5) + col % 8, col // 8
+    spot, place = 8 * me_x + row % 16, 8 * (slot // cores) + cell
+    valid = (slot % cores == row // 80) & (col % 8 < 2) & (cell < 9) & (place < 8 * across_x)
+    valid = valid & (row % 16 < 9) & (spot < 8 * across_x)
+    GX[...] = jnp.where(valid, gauss(spot - place, 8 * across_x), 0.0)
+    r, c = iota((2 * CZ, 3 * CZ), 0), iota((2 * CZ, 3 * CZ), 1)
+    PX[...] = (r % CZ == 8 * (c // CZ) + c % 8).astype(F32).astype(BF16)
+    row, col = iota((CY, 8 * chips), 0), iota((CY, 8 * chips), 1)
+    place = 2 * (cores * (col // 8) + (col % 8) // 3) + (col % 8) % 3
+    valid = (col % 8 < 3 * cores) & (place < 2 * across_y)
+    along = jnp.zeros((CY, 8 * chips), F32)
+    for y in range(3):
+        spot = 2 * me_y + y
+        share = jnp.maximum(0, 16 - jnp.abs(row - 16 * y)).astype(F32) / 16.0
+        term = jnp.where(valid & (spot < 2 * across_y), gauss(spot - place, 2 * across_y), 0.0)
+        along = along + share * term
+    GY[...] = along
+    few.wait()
+    WZ[...] = stacked(coarse_z(taps))
+    W0[...] = stacked(toeplitz(taps, 0, (CZ, CZ), iota((CZ, CZ), 0) - iota((CZ, CZ), 1)))
 
     def remote(src, dst, send, recv, **target):
         return pltpu.make_async_remote_copy(
@@ -201,17 +232,38 @@
 
     y0_up = remote(q.at[:, pl.ds(CY - 4, 4)], E.at[:, pl.ds(4, 4)], y0_send.at[0], y0_recv.at[0], gy=above_y)
     y0_down = remote(q.at[:, pl.ds(0, 4)], E.at[:, pl.ds(40, 4)], y0_send.at[1], y0_recv.at[1], gy=below_y)
-    for load in loads:
-        load.wait()
-
-    T1[0, 8:40, :] = 2.0 * E[0, 8:40, :] + E[1, 8:40, :]
+    def down_x(i, carry):
+        load(i).wait()
+        for t in range(4):
+            rows = pl.ds(8 + 8 * t, 8)
+            value = E[pl.ds(16 * i, 16), rows, :]
+            before = E[jnp.maximum(16 * i - 1, 0), rows, :]
+            before = jnp.where(i > 0, before, 0.0)
+            for k in range(8):
+                T1[8 * i + k, rows, :] = (before if k == 0 else value[2 * k - 1]) + 2.0 * value[2 * k] + value[2 * k + 1]
+            running = value[15]
+            rising = running
+            for k in range(14, 0, -1):
+                running = running + value[k]
+                rising = rising + running
+            fine = pl.ds(8 * t, 8)
+            X4[i, fine, :] = X4[i, fine, :] + (16.0 * (running + value[0]) - rising)
+            X4[i + 1, fine, :] = rising
+        return carry
+
+    lax.fori_loop(0, CX // 16, down_x, 0)
     T1[64, 8:40, :] = E[CX - 1, 8:40, :]
 
-    def down_x(i, carry):
-        T1[i, 8:40, :] = E[2 * i - 1, 8:40, :] + 2.0 * E[2 * i, 8:40, :] + E[2 * i + 1, 8:40, :]
-        return carry
-
-    lax.fori_loop(1, 64, down_x, 0, unroll=3)
+    value = product(X4[...].reshape(9 * CY, CZ), Z4[...]) * K4[...]
+    pick = ((iota((8, 9 * CY), 1) // CY) % 2 == iota((8, 9 * CY), 0)).astype(F32)
+    mine = me_x * cores + core
+    GA[mine, 0:2, :] = picked(pick, value)[0:2]
+    pl.semaphore_wait(barrier, len(around + near_by + far_off))
+    two = pl.ds(0, 2)
+    for x, y in near_by:
+        remote(GA.at[mine, two], GA.at[mine, two], ga_send, ga_recv, gx=x, gy=y).start()
+    pl.when(jnp.logical_not(last_y))(y0_up.start)
+    pl.when(jnp.logical_not(first_y))(y0_down.start)
 
     def down_y(i, carry):
         R1[i + 1] = (
@@ -219,40 +271,21 @@
         )
         return carry
 
-    lax.fori_loop(0, 65, down_y, 0, unroll=5)
-
-    pl.semaphore_wait(barrier, len(around + near_by + far_off))
-    pl.when(jnp.logical_not(last_y))(y0_up.start)
-    pl.when(jnp.logical_not(first_y))(y0_down.start)
-    for level in (2, 3, 4):
+    lax.fori_loop(0, 65, down_y, 0, unroll=13)
+
+    for level in (2, 3):
         finer, mid, n = R[level - 1], T[level], NXL[level]
         inner, rows = ROWS[level - 1], ROWS[level]
         pairs = finer[1 : 2 * n + 1].reshape(n, 2, inner, CZ)
         before = finer[0 : 2 * n].reshape(n, 2, inner, CZ)
         mid[0:n, 8 : 8 + inner, :] = before[:, 0] + 2.0 * pairs[:, 0] + pairs[:, 1]
         mid[n, 8 : 8 + inner, :] = finer[2 * n] + 2.0 * finer[2 * n + 1]
-        value = (
+        R[level][1 : n + 2] = (
             mid[:, pl.ds(7, rows, stride=2), :]
             + 2.0 * mid[:, pl.ds(8, rows, stride=2), :]
             + mid[:, pl.ds(9, rows, stride=2), :]
         )
-        if level < 4:
-            R[level][1 : n + 2] = value
-
-    value = jnp.dot(value.reshape(72, CZ), Z4[...], precision=HIGHEST, preferred_element_type=F32)
-    row, lane = iota((72, CZ), 0), iota((72, CZ), 1)
-    value = jnp.where((lane // 8 == 3 * (row // 16) + row % 8) & (row % 8 < 3), value, 0.0)
-    pick = ((iota((8, 72), 1) // 8) % 2 == iota((8, 72), 0)).astype(F32)
-    mine = me_x * cores + core
-    GA[mine, 0:2, :] = jnp.dot(pick, value, precision=HIGHEST, preferred_element_type=F32)[0:2]
-    two = pl.ds(0, 2)
-    for x, y in near_by:
-        remote(GA.at[mine, two], GA.at[mine, two], ga_send, ga_recv, gx=x, gy=y).start()
-
-
-    few.wait()
-    WZ[...] = stacked(coarse_z(taps))
-    W0[...] = stacked(toeplitz(taps, 0, (CZ, CZ), iota((CZ, CZ), 0) - iota((CZ, CZ), 1)))
+
     A1[4:69] = product(R1[1:67].reshape(66 * 24, CZ), WZ[...]).reshape(66, 24, CZ)[0:65]
     A2[4:37] = product(R2[1:34].reshape(33 * 16, CZ), WZ[...]).reshape(33, 16, CZ)
     A3[4:21] = product(R3[1:19].reshape(18 * 8, CZ), WZ[...]).reshape(18, 8, CZ)[0:17]
@@ -283,7 +316,22 @@
         C[4 + i, 8:24, :] = weighted([E[i, 12 + k : 28 + k, :] for k in range(9)], w0)
         return carry
 
-    lax.fori_loop(0, CX, mid_y, 0, unroll=2)
+    def outer_y(i, carry):
+        C[4 + i, 0:8, :] = weighted([E[i, 4 + k : 12 + k, :] for k in range(9)], w0)
+        C[4 + i, 24:32, :] = weighted([E[i, 28 + k : 36 + k, :] for k in range(9)], w0)
+        return carry
+
+    def finest_x(i, tiles):
+        for t in tiles:
+            rows = pl.ds(8 * t, 8)
+            value = C[pl.ds(16 * i, 24), rows, :]
+            out[pl.ds(16 * i, 16), rows, :] = weighted([value[k : k + 16] for k in range(9)], w0)
+
+    def finest_z(first, count):
+        at = pl.ds(first, count)
+        out[at] = product(out[at].reshape(count * CY, CZ), W0[...]).reshape(count, CY, CZ)
+
+    lax.fori_loop(0, CX, mid_y, 0, unroll=8)
 
     pl.when(jnp.logical_not(first_x))(cx_up.wait_recv)
     pl.when(jnp.logical_not(last_x))(cx_down.wait_recv)
@@ -299,7 +347,7 @@
             target[i, pl.ds(8, rows), :] = weighted([array[i + k] for k in range(9)], wl)
             return carry
 
-        lax.fori_loop(0, n + 1, along_x, 0, unroll={1: 5, 2: 3, 3: 1}[level])
+        lax.fori_loop(0, n + 1, along_x, 0, unroll={1: 5, 2: 11, 3: 17}[level])
 
         @pl.when(last_x)
         def _(target=B[level], rows=rows, n=n):
@@ -335,61 +383,47 @@
     pl.when(jnp.logical_not(first_y))(y0_up.wait_recv)
     pl.when(jnp.logical_not(last_y))(y0_down.wait_recv)
 
-    def outer_y(i, carry):
-        C[4 + i, 0:8, :] = weighted([E[i, 4 + k : 12 + k, :] for k in range(9)], w0)
-        C[4 + i, 24:32, :] = weighted([E[i, 28 + k : 36 + k, :] for k in range(9)], w0)
-        return carry
-
-    lax.fori_loop(0, 4, outer_y, 0, unroll=2)
-    lax.fori_loop(CX - 4, CX, outer_y, 0, unroll=2)
+    lax.fori_loop(0, 4, outer_y, 0, unroll=4)
+    lax.fori_loop(CX - 4, CX, outer_y, 0, unroll=4)
     x0_up = remote(C.at[pl.ds(CX, 4)], C.at[pl.ds(0, 4)], x0_send.at[0], x0_recv.at[0], gx=above_x)
     x0_down = remote(C.at[pl.ds(4, 4)], C.at[pl.ds(CX + 4, 4)], x0_send.at[1], x0_recv.at[1], gx=below_x)
     pl.when(jnp.logical_not(last_x))(x0_up.start)
     pl.when(jnp.logical_not(first_x))(x0_down.start)
 
-    lax.fori_loop(4, CX - 4, outer_y, 0, unroll=2)
-
-    row, col = iota((cores * 80, 8 * across_x * cores), 0), iota((cores * 80, 8 * across_x * cores), 1)
-    cell, slot = 2 * ((row // 16) % 5) + col % 8, col // 8
-    spot, place = 8 * me_x + row % 16, 8 * (slot // cores) + cell
-    valid = (slot % cores == row // 80) & (col % 8 < 2) & (cell < 9) & (place < 8 * across_x)
-    valid = valid & (row % 16 < 9) & (spot < 8 * across_x)
-    along = jnp.where(valid, gauss(spot - place, 8 * across_x), 0.0)
-    r, c = iota((CZ, 3 * CZ), 0), iota((CZ, 3 * CZ), 1)
-    pick = (r == 8 * (c // CZ) + c % 8).astype(F32)
     row, col = iota((8, 48 * cores), 0), iota((8, 48 * cores), 1)
     gather = ((row // 3 == (col // 16) % cores) & (row % 3 == col // (16 * cores))).astype(F32)
     drain(GA, across_x * cores - 1, 2, ga_recv)
-    value = jnp.dot(along, GA[...].reshape(8 * across_x * cores, CZ), precision=HIGHEST, preferred_element_type=F32)
+    value = general(GX[...], GA[...].reshape(8 * across_x * cores, CZ))
     value = value.reshape(cores, 5, 16, CZ)
     lane = iota((cores, 16, CZ), 2)
     total = jnp.where(lane < 24, value[:, 0], 0.0)
     for g in range(1, 5):
         total = total + jnp.where(lane < 24, pltpu.roll(value[:, g], CZ - 24 * g, 2), 0.0)
-    value = jnp.dot(total.reshape(cores * 16, CZ), pick, precision=HIGHEST, preferred_element_type=F32)
+    both = jnp.concatenate(split(total.reshape(cores * 16, CZ)), axis=1)
+    value = jnp.dot(both, PX[...], preferred_element_type=F32)
     row, lane = iota((cores * 16, CZ), 0), iota((cores * 16, CZ), 1)
     keep = (lane // 8 == row % 16) & (lane < 72)
     value = jnp.concatenate([jnp.where(keep, value[:, y * CZ : y * CZ + CZ], 0.0) for y in range(3)], axis=0)
     here = me_y // cores
-    GB[here] = jnp.dot(gather, value, precision=HIGHEST, preferred_element_type=F32)
+    GB[here] = picked(gather, value)
     six = pl.ds(0, 6)
     for x, y in far_off:
         remote(GB.at[here, six], GB.at[here, six], gb_send, gb_recv, gy=y).start()
 
+    lax.fori_loop(4, CX - 4, outer_y, 0, unroll=6)
+
+    lax.fori_loop(1, CX // 16 - 1, lambda i, c: (finest_x(i, (1, 2)), c)[1], 0)
+
+    lax.fori_loop(1, CX // 16 - 1, lambda i, c: (finest_x(i, (0, 3)), c)[1], 0)
+
+    finest_z(16, CX - 32)
+
     pl.when(jnp.logical_not(first_x))(x0_up.wait_recv)
     pl.when(jnp.logical_not(last_x))(x0_down.wait_recv)
-
-    def finest_x(i, carry):
-        w0 = [taps[0, k] for k in range(2 * REACH + 1)]
-        for t in range(4):
-            rows = pl.ds(8 * t, 8)
-            value = C[pl.ds(16 * i, 24), rows, :]
-            out[pl.ds(16 * i, 16), rows, :] = weighted([value[k : k + 16] for k in range(9)], w0)
-        return carry
-
-    lax.fori_loop(0, CX // 16, finest_x, 0)
-
-    out[...] = product(out[...].reshape(CX * CY, CZ), W0[...]).reshape(CX, CY, CZ)
+    finest_x(0, range(4))
+    finest_x(CX // 16 - 1, range(4))
+    finest_z(0, 16)
+    finest_z(CX - 16, 16)
 
     pl.when(jnp.logical_not(first_y))(cy_up.wait_recv)
     pl.when(jnp.logical_not(last_y))(cy_down.wait_recv)
@@ -409,7 +443,7 @@
             target[x] = weighted([array[x, 4 + k : 4 + k + rows, :] for k in range(9)], wl)
             return carry
 
-        lax.fori_loop(0, count, along_y, 0, unroll={1: 5, 2: 3, 3: 1}[level])
+        lax.fori_loop(0, count, along_y, 0, unroll={1: 5, 2: 11, 3: 17}[level])
 
         @pl.when(last_y)
         def _(target=U[level], n=n, count=count):
@@ -443,7 +477,7 @@
         G0[x, pl.ds(1, 16, stride=2), :] = 0.5 * (low + high)
         return carry
 
-    lax.fori_loop(0, 65, rise_y, 0, unroll=5)
+    lax.fori_loop(0, 65, rise_y, 0, unroll=13)
 
     def finish(i, carry):
         low, high = G0[i], G0[i + 1]
@@ -451,19 +485,10 @@
         out[2 * i + 1] = out[2 * i + 1] + 0.5 * (low + high)
         return carry
 
-    lax.fori_loop(0, CX // 2, finish, 0, unroll=2)
-
-    row, col = iota((CY, 8 * chips), 0), iota((CY, 8 * chips), 1)
-    place = 2 * (cores * (col // 8) + (col % 8) // 3) + (col % 8) % 3
-    valid = (col % 8 < 3 * cores) & (place < 2 * across_y)
-    along = jnp.zeros((CY, 8 * chips), F32)
-    for y in range(3):
-        spot = 2 * me_y + y
-        share = jnp.maximum(0, 16 - jnp.abs(row - 16 * y)).astype(F32) / 16.0
-        term = jnp.where(valid & (spot < 2 * across_y), gauss(spot - place, 2 * across_y), 0.0)
-        along = along + share * term
+    lax.fori_loop(0, CX // 2, finish, 0, unroll=4)
+
     drain(GB, chips - 1, 6, gb_recv)
-    value = jnp.dot(along, GB[...].reshape(8 * chips, CZ), precision=HIGHEST, preferred_element_type=F32)
+    value = general(GY[...], GB[...].reshape(8 * chips, CZ))
     lane = iota((CY, CZ), 1)
     spread = jnp.concatenate([jnp.where(lane // 8 == x, value, 0.0) for x in range(9)], axis=0)
     high, low = split(spread)
@@ -514,7 +539,7 @@
         pltpu.SMEM((4, 9), F32),
         vmem(CX, 48, CZ),
         vmem(CX + 8, CY, CZ),
-        vmem(65, 56, CZ), vmem(33, 40, CZ), vmem(17, 24, CZ), vmem(9, 24, CZ),
+        vmem(65, 56, CZ), vmem(33, 40, CZ), vmem(17, 24, CZ), vmem(9, CY, CZ),
         vmem(67, 24, CZ), vmem(35, 16, CZ), vmem(19, 8, CZ),
         vmem(73, 24, CZ), vmem(41, 16, CZ), vmem(25, 8, CZ),
         vmem(65, 40, CZ), vmem(33, 32, CZ), vmem(17, 24, CZ),
@@ -524,8 +549,10 @@
         vmem(2, 65, 8, CZ), vmem(2, 65, 8, CZ),
         vmem(across_x * cores, 8, CZ), vmem(across_y // cores, 8, CZ),
         vmem(2 * CZ, 2 * CZ, dtype=BF16), vmem(2 * CZ, 2 * CZ, dtype=BF16), vmem(2 * CZ, CZ, dtype=BF16), vmem(2 * CZ, CZ, dtype=BF16),
-        vmem(CZ, CZ), vmem(66, 24, CZ),
-        single, pltpu.SemaphoreType.DMA((4,)),
+        vmem(2 * CZ, 2 * CZ, dtype=BF16), vmem(9 * CY, CZ),
+        vmem(cores * 80, 8 * across_x * cores), vmem(2 * CZ, 3 * CZ, dtype=BF16), vmem(CY, 8 * across_y // cores),
+        vmem(66, 24, CZ),
+        single, pltpu.SemaphoreType.DMA((CX // 16,)),
         pair, pair, pair, pair, pair, pair, pair, pair, pair, pair,
         single, single, single, single,
     ]

time: 24.7 us -> 23.6 us (0.955)
  Pallas kernels: 24.5 us -> 23.5 us
    pallas_call x1, Pallas kernels: 23.1 us -> 22.1 us  [local(): pl.pallas_call(functools.partial(kernel, across_x, across_y), out_shape=[...]
where the time goes in v5:
time: 23.6 us
  Pallas kernels  23.5 us (100%)
    pallas_call x1, Pallas kernels, local(): pl.pallas_call(functools.partial(kernel, across_x, across_y), out_shape=[...  22.1 us
    pallas_call x1, Pallas kernels, local(): pl.pallas_call(last, out_shape=jax.ShapeDtypeStruct((CX, CY, CZ), F32), i...  1.4 us

profile of v5, /device:TPU:1, one launch (start us, length us, event | category | flops | bytes accessed | tf_op | source)
XLA Modules:
  0.0 23.6 jit_solution(17406973482043330977)
XLA Ops:
  0.0 22.1 %shard_map.28 = (f32[128,32,128]{2,1,0:T(8,128)S(1)}, f32[8,32,128]{2,1,0:T(8,128)S(1)}, f32[8,32,128]{2,1,0:T(8,128)S(1)}) custom-call(f32[4,9]{1,0:T(4,128)} %taps_in.1, f32[128,32,128]{2,1,0:T(8,128)} %q.1), custom_call_target="tpu_custom_call" | custom-call | tf_op jit(solution)/shard_map/pallas_call | solution.py:561
  22.2 1.4 %shard_map.29 = f32[128,32,128]{2,1,0:T(8,128)} custom-call(f32[128,32,128]{2,1,0:T(8,128)S(1)} %get-tuple-element.8.fine, f32[8,32,128]{2,1,0:T(8,128)S(1)} %get-tuple-element.9.coarse, f32[8,32,128]{2,1,0:T(8,128)S(1)} %get-tuple-element.10.slope), custom_call_target="tpu_custom_call" | custom-call | tf_op jit(solution)/shard_map/pallas_call | solution.py:571

commit v6 on v5

--- a/solution.py
+++ b/solution.py
@@ -130,7 +130,7 @@
         (lax.rem(me_x + x, across_x), me_y - core + lax.rem(core + c, cores))
         for x in range(across_x) for c in range(cores) if x or c
     ]
-    far_off = [(me_x, lax.rem(me_y + cores * step, across_y)) for step in range(1, chips)]
+    far_off = [(me_x, lax.rem(me_y + cores * step, across_y)) for step in sorted(range(1, chips), key=lambda step: abs(2 * step - chips))]
     steps = (1, 2, across_y - 2, across_y - 1) if across_y > 4 else ()
     around = [(me_x, lax.rem(me_y + step, across_y)) for step in steps]
     barrier = pltpu.get_barrier_semaphore()
@@ -150,6 +150,7 @@
         blank(B[level], NXL[level] + 1, (0, 8), *(((16, 8),) if level == 3 else ()))
         rows = ROWS[level]
         R[level][0] = jnp.zeros((rows, CZ), F32)
+    XR[:, :, 17:24, :] = jnp.zeros((2, 5, 7, CZ), F32)
     GA[:, 2:8, :] = jnp.zeros((across_x * cores, 6, CZ), F32)
     GB[:, 6:8, :] = jnp.zeros((chips, 2, CZ), F32)
 
@@ -305,8 +306,9 @@
             XS[way, i, 0:16, :] = jnp.where(lane >= 64, A2[at[2]], XS[way, i, 0:16, :])
             lane = iota((8, CZ), 1)
             XS[way, i, 0:8, :] = jnp.where(lane >= 96, A3[at[3]], XS[way, i, 0:8, :])
-    cx_up = remote(XS.at[0], XR.at[0], cx_send.at[0], cx_recv.at[0], gx=above_x)
-    cx_down = remote(XS.at[1], XR.at[1], cx_send.at[1], cx_recv.at[1], gx=below_x)
+    used = pl.ds(0, 17)
+    cx_up = remote(XS.at[0, :, used], XR.at[0, :, used], cx_send.at[0], cx_recv.at[0], gx=above_x)
+    cx_down = remote(XS.at[1, :, used], XR.at[1, :, used], cx_send.at[1], cx_recv.at[1], gx=below_x)
     pl.when(jnp.logical_not(last_x))(cx_up.start)
     pl.when(jnp.logical_not(first_x))(cx_down.start)
 

time: 23.6 us -> 23.4 us (level)
    pallas_call x1, Pallas kernels: 22.1 us -> 21.9 us  [local(): pl.pallas_call(functools.partial(kernel, across_x, across_y), out_shape=[...]
where the time goes in v6:
time: 23.4 us; the launch traced here: 23.3 us
  Pallas kernels  23.3 us (100%)
    pallas_call x1, Pallas kernels, local(): pl.pallas_call(functools.partial(kernel, across_x, across_y), out_shape=[...  21.9 us
    pallas_call x1, Pallas kernels, local(): pl.pallas_call(last, out_shape=jax.ShapeDtypeStruct((CX, CY, CZ), F32), i...  1.4 us

profile of v6, /device:TPU:1, one launch (start us, length us, event | category | flops | bytes accessed | tf_op | source)
XLA Modules:
  0.0 23.3 jit_solution(12021899997693695695)
XLA Ops:
  0.0 21.9 %shard_map.28 = (f32[128,32,128]{2,1,0:T(8,128)S(1)}, f32[8,32,128]{2,1,0:T(8,128)S(1)}, f32[8,32,128]{2,1,0:T(8,128)S(1)}) custom-call(f32[4,9]{1,0:T(4,128)} %taps_in.1, f32[128,32,128]{2,1,0:T(8,128)} %q.1), custom_call_target="tpu_custom_call" | custom-call | tf_op jit(solution)/shard_map/pallas_call | solution.py:563
  21.9 1.4 %shard_map.29 = f32[128,32,128]{2,1,0:T(8,128)} custom-call(f32[128,32,128]{2,1,0:T(8,128)S(1)} %get-tuple-element.8.fine, f32[8,32,128]{2,1,0:T(8,128)S(1)} %get-tuple-element.9.coarse, f32[8,32,128]{2,1,0:T(8,128)S(1)} %get-tuple-element.10.slope), custom_call_target="tpu_custom_call" | custom-call | tf_op jit(solution)/shard_map/pallas_call | solution.py:573

commit v7 on v6

--- a/solution.py
+++ b/solution.py
@@ -287,7 +287,12 @@
             + mid[:, pl.ds(9, rows, stride=2), :]
         )
 
-    A1[4:69] = product(R1[1:67].reshape(66 * 24, CZ), WZ[...]).reshape(66, 24, CZ)[0:65]
+    def level_1(first, count, kept):
+        value = product(R1[first + 1 : first + count + 1].reshape(count * 24, CZ), WZ[...])
+        A1[first + 4 : first + kept + 4] = value.reshape(count, 24, CZ)[0:kept]
+
+    level_1(0, 6, 5)
+    level_1(60, 6, 5)
     A2[4:37] = product(R2[1:34].reshape(33 * 16, CZ), WZ[...]).reshape(33, 16, CZ)
     A3[4:21] = product(R3[1:19].reshape(18 * 8, CZ), WZ[...]).reshape(18, 8, CZ)[0:17]
 
@@ -311,6 +316,7 @@
     cx_down = remote(XS.at[1, :, used], XR.at[1, :, used], cx_send.at[1], cx_recv.at[1], gx=below_x)
     pl.when(jnp.logical_not(last_x))(cx_up.start)
     pl.when(jnp.logical_not(first_x))(cx_down.start)
+    level_1(5, 56, 55)
 
     w0 = [taps[0, k] for k in range(2 * REACH + 1)]
 

time: 23.4 us -> 23.4 us (level)
  no operation moved by 1% of the time
where the time goes in v7:
time: 23.4 us; the launch traced here: 23.3 us
  Pallas kernels  23.3 us (100%)
    pallas_call x1, Pallas kernels, local(): pl.pallas_call(functools.partial(kernel, across_x, across_y), out_shape=[...  21.9 us
    pallas_call x1, Pallas kernels, local(): pl.pallas_call(last, out_shape=jax.ShapeDtypeStruct((CX, CY, CZ), F32), i...  1.4 us

profile of v7, /device:TPU:1, one launch (start us, length us, event | category | flops | bytes accessed | tf_op | source)
XLA Modules:
  0.0 23.3 jit_solution(634943517353018904)
XLA Ops:
  0.0 21.9 %shard_map.28 = (f32[128,32,128]{2,1,0:T(8,128)S(1)}, f32[8,32,128]{2,1,0:T(8,128)S(1)}, f32[8,32,128]{2,1,0:T(8,128)S(1)}) custom-call(f32[4,9]{1,0:T(4,128)} %taps_in.1, f32[128,32,128]{2,1,0:T(8,128)} %q.1), custom_call_target="tpu_custom_call" | custom-call | tf_op jit(solution)/shard_map/pallas_call | solution.py:569
  21.9 1.4 %shard_map.29 = f32[128,32,128]{2,1,0:T(8,128)} custom-call(f32[128,32,128]{2,1,0:T(8,128)S(1)} %get-tuple-element.8.fine, f32[8,32,128]{2,1,0:T(8,128)S(1)} %get-tuple-element.9.coarse, f32[8,32,128]{2,1,0:T(8,128)S(1)} %get-tuple-element.10.slope), custom_call_target="tpu_custom_call" | custom-call | tf_op jit(solution)/shard_map/pallas_call | solution.py:579
